TPU v7x, 32 devices: a whole 2x2x4 slice. The times are simulated.
32 devices in a mesh: wide: 16 (over z, y, x), narrow: 2 (over core).
Axes of the slice: x: 2, y: 2, z: 4, core: 2. Of those that a mesh axis runs over, the one named last changes fastest.
Arguments:
- user_table: bfloat16 [65536, 256], P('wide'), may hold values from -3 to 3
- item_table: bfloat16 [32768, 256], P('wide'), may hold values from -3 to 3
- week_table: bfloat16 [1024, 256], P('wide'), may hold values from -3 to 3
- profile: bfloat16 [65536, 4096], P('wide', 'narrow'), may hold values from -6 to 6
- feature_table: bfloat16 [4096, 256], P('narrow'), may hold values from -0.375 to 0.375
- user_req: int32 [32, 16, 32], P(('wide', 'narrow')), may hold values from 0 to 4095
- item_req: int32 [32, 16, 32], P(('wide', 'narrow')), may hold values from 0 to 2047
- week_req: int32 [32, 16, 4], P(('wide', 'narrow')), may hold values from 0 to 63
- user_counts: int32 [32, 16], P(('wide', 'narrow')), may hold values from 1 to 32, 256 in all within a row
- item_counts: int32 [32, 16], P(('wide', 'narrow')), may hold values from 1 to 32, 256 in all within a row
- week_counts: int32 [32, 16], P(('wide', 'narrow')), may hold values from 1 to 4, 28 in all within a row
- pos_cells: int32 [32, 4096], P(('wide', 'narrow')), may hold values from 0 to 1835007
Outputs:
- grad_users: float32 [65536, 256], P(('wide', 'narrow'))
- grad_items: float32 [32768, 256], P(('wide', 'narrow'))
- grad_weeks: float32 [1024, 256], P(('wide', 'narrow'))
- grad_features: float32 [4096, 256], P('narrow')
Inputs may be any that keep to these rules, and one draw needn't show every extreme that they name: `user_req`: only the first user_counts[d, o] slots of owner o are read; the rest hold arbitrary row numbers. Rows may repeat. `item_req`: only the first item_counts[d, o] slots of owner o are read. `week_req`: only the first week_counts[d, o] slots of owner o are read. `user_counts`: each block's counts sum to 256; every block has an owner with exactly 32. `item_counts`: each block's counts sum to 256; every block has an owner with exactly 32. `week_counts`: each block's counts sum to 28; every block has an owner with exactly 4. `pos_cells`: cells may repeat.
All inputs are finite; a program needn't handle non-finite values.
Results may differ from a plain program's by a relative error of at most 0.0015.
Values may be sent and summed in bfloat16 or wider, within the bound.
No kernel may reach another device: no remote copies, remote signals or barrier semaphores. Data moves between devices by JAX's collectives and lax.ppermute only.
A program may use at most 128 MiB of HBM per device.

v0:
```python
import jax
import jax.numpy as jnp
from jax import lax
from jax.sharding import PartitionSpec as P

RANK = 256
BU = 256
BI = 256
BW = 28
CAPU = 32
CAPI = 32
CAPW = 4


def compact_index(counts, cap, total):
    ends = jnp.cumsum(counts)
    starts = ends - counts
    place = jnp.arange(total, dtype=jnp.int32)
    owner = jnp.sum((ends[None, :] <= place[:, None]).astype(jnp.int32), axis=1)
    onehot = (owner[:, None] == jnp.arange(counts.shape[0], dtype=jnp.int32)[None, :]).astype(
        jnp.int32
    )
    first = jnp.sum(onehot * starts[None, :], axis=1)
    return owner * cap + place - first


def block_grads(user_rows, item_rows, week_rows, pos):
    nweek, nuser, nitem = (week_rows.shape[0], user_rows.shape[0], item_rows.shape[0])
    user_f = user_rows.astype(jnp.float32)
    week_f = week_rows.astype(jnp.float32)
    mixed = (user_f[None] * week_f[:, None]).astype(jnp.bfloat16)
    model = jnp.einsum("kir,jr->kij", mixed, item_rows, preferred_element_type=jnp.float32)
    cells = nweek * nuser * nitem
    cpos = jnp.zeros((cells,), jnp.float32).at[pos].set(1.0).reshape(nweek, nuser, nitem)
    resid = (jax.nn.sigmoid(model) - cpos).astype(jnp.bfloat16)
    partial_value = jnp.einsum("kij,jr->kir", resid, item_rows, preferred_element_type=jnp.float32)
    grad_u = jnp.sum(partial_value * week_f[:, None, :], axis=0)
    grad_w = jnp.sum(partial_value * user_f[None], axis=1)
    grad_v = jnp.einsum("kij,kir->jr", resid, mixed, preferred_element_type=jnp.float32)
    return (grad_u, grad_v, grad_w)


def into_slots(grads, flat, owners, cap):
    slots = jnp.zeros((owners * cap, grads.shape[1]), jnp.float32).at[flat].set(grads)
    return slots.reshape(owners, cap, grads.shape[1])


def local(
    user_table,
    item_table,
    week_table,
    profile,
    feature_table,
    user_req,
    item_req,
    week_req,
    user_counts,
    item_counts,
    week_counts,
    pos_cells,
):
    owners = lax.axis_size("wide")
    shares = lax.axis_size("narrow")
    user_need, item_need, week_need = (user_req[0], item_req[0], week_req[0])
    user_flat = compact_index(user_counts[0], CAPU, BU)
    item_flat = compact_index(item_counts[0], CAPI, BI)
    week_flat = compact_index(week_counts[0], CAPW, BW)
    own_users, own_items, own_weeks = (
        user_table.shape[0],
        item_table.shape[0],
        week_table.shape[0],
    )
    got_u, got_v, got_w = (
        lax.all_to_all(user_need, "wide", split_axis=0, concat_axis=0, tiled=True),
        lax.all_to_all(item_need, "wide", split_axis=0, concat_axis=0, tiled=True),
        lax.all_to_all(week_need, "wide", split_axis=0, concat_axis=0, tiled=True),
    )
    back_u, back_v, back_w = (
        lax.all_to_all(user_table[got_u], "wide", split_axis=0, concat_axis=0, tiled=True),
        lax.all_to_all(item_table[got_v], "wide", split_axis=0, concat_axis=0, tiled=True),
        lax.all_to_all(week_table[got_w], "wide", split_axis=0, concat_axis=0, tiled=True),
    )
    week_rows = back_w.reshape(-1, RANK)[week_flat]
    user_rows = back_u.reshape(-1, RANK)[user_flat]
    item_rows = back_v.reshape(-1, RANK)[item_flat]
    grad_u, grad_v, grad_w = block_grads(user_rows, item_rows, week_rows, pos_cells[0])
    slots_u = into_slots(grad_u, user_flat, owners, CAPU)
    slots_v = into_slots(grad_v, item_flat, owners, CAPI)
    slots_w = into_slots(grad_w, week_flat, owners, CAPW)
    ret_u, ret_v, ret_w = (
        lax.all_to_all(slots_u, "wide", split_axis=0, concat_axis=0, tiled=True),
        lax.all_to_all(slots_v, "wide", split_axis=0, concat_axis=0, tiled=True),
        lax.all_to_all(slots_w, "wide", split_axis=0, concat_axis=0, tiled=True),
    )
    dense_w = (
        jnp.zeros((own_weeks, RANK), jnp.float32).at[got_w.reshape(-1)].add(ret_w.reshape(-1, RANK))
    )
    dense_u = (
        jnp.zeros((own_users, RANK), jnp.float32).at[got_u.reshape(-1)].add(ret_u.reshape(-1, RANK))
    )
    dense_v = (
        jnp.zeros((own_items, RANK), jnp.float32).at[got_v.reshape(-1)].add(ret_v.reshape(-1, RANK))
    )
    model = lax.dot_general(
        user_table, feature_table, (((1,), (1,)), ((), ())), preferred_element_type=jnp.float32
    )
    resid = (model - profile.astype(jnp.float32)).astype(jnp.bfloat16)
    dense_u = dense_u + 0.0625 * jnp.dot(resid, feature_table, preferred_element_type=jnp.float32)
    feat_terms = 0.0625 * lax.dot_general(
        resid, user_table, (((0,), (0,)), ((), ())), preferred_element_type=jnp.float32
    )
    grad_features = lax.psum(feat_terms, "wide")
    total_u, total_v, total_w = lax.psum((dense_u, dense_v, dense_w), "narrow")
    place = lax.axis_index("narrow")
    grad_users = lax.dynamic_slice_in_dim(
        total_u, place * (own_users // shares), own_users // shares, 0
    )
    grad_items = lax.dynamic_slice_in_dim(
        total_v, place * (own_items // shares), own_items // shares, 0
    )
    grad_weeks = lax.dynamic_slice_in_dim(
        total_w, place * (own_weeks // shares), own_weeks // shares, 0
    )
    return (grad_users, grad_items, grad_weeks, grad_features)


def solution(mesh):
    return jax.shard_map(
        local,
        mesh=mesh,
        in_specs=(
            P("wide", None),
            P("wide", None),
            P("wide", None),
            P("wide", "narrow"),
            P("narrow", None),
            P(("wide", "narrow"), None, None),
            P(("wide", "narrow"), None, None),
            P(("wide", "narrow"), None, None),
            P(("wide", "narrow"), None),
            P(("wide", "narrow"), None),
            P(("wide", "narrow"), None),
            P(("wide", "narrow"), None),
        ),
        out_specs=(
            P(("wide", "narrow"), None),
            P(("wide", "narrow"), None),
            P(("wide", "narrow"), None),
            P("narrow", None),
        ),
        check_vma=False,
    )
```

profile of v0, /device:TPU:0, one launch (start us, length us, event | category | flops | bytes accessed | tf_op | source)
XLA Modules:
  0.0 360.4 jit_solution(6467091366148281950)
XLA Ops:
  7.2 1.5 copy.36
  8.7 8.3 %all-to-all-start.2 = ((s32[16,1,4]{2,1,0:T(1,128)}), s32[16,1,4]{2,1,0:T(1,128)S(1)}, u32[]{:S(2)}, u32[]{:S(2)}) async-start(s32[16,1,4]{2,1,0:T(1,128)} %copy.36), calls=%async_computation.2 | async-start | bytes 16384 | tf_op jit(solution)/shard_map/all_to_all | solution.py:76
  17.0 0.7 copy.39
  18.7 0.7 copy.40
  20.3 0.7 copy.35
  21.9 0.7 compare_select_fusion
  22.8 1.4 all-to-all-done.2
  24.2 5.5 %all-to-all-start = ((s32[16,1,32]{2,1,0:T(1,128)}), s32[16,1,32]{2,1,0:T(1,128)S(1)}, u32[]{:S(2)}, u32[]{:S(2)}) async-start(s32[16,1,32]{2,1,0:T(1,128)} %bitcast.95), calls=%async_computation | async-start | bytes 16384 | tf_op jit(solution)/shard_map/all_to_all | solution.py:74
  30.0 1.4 gather_fusion.2
  32.0 4.9 %all-to-all-done = s32[16,1,32]{2,1,0:T(1,128)S(1)} async-done(((s32[16,1,32]{2,1,0:T(1,128)}), s32[16,1,32]{2,1,0:T(1,128)S(1)}, u32[]{:S(2)}, u32[]{:S(2)}) %all-to-all-start) | async-done | bytes 2080 | tf_op jit(solution)/shard_map/all_to_all | solution.py:74
  36.9 3.5 all-to-all-start.4
  40.5 7.1 %all-to-all-done.4 = s32[16,1,32]{2,1,0:T(1,128)S(1)} async-done(((s32[16,1,32]{2,1,0:T(1,128)}), s32[16,1,32]{2,1,0:T(1,128)S(1)}, u32[]{:S(2)}, u32[]{:S(2)}) %all-to-all-start.4) | async-done | bytes 2080 | tf_op jit(solution)/shard_map/all_to_all | solution.py:75
  47.5 3.5 all-to-all-start.3
  51.1 2.6 gather_fusion
  53.7 4.8 %all-to-all-done.3 = bf16[16,4,256]{2,1,0:T(4,128)(2,1)S(1)} async-done(((bf16[16,4,256]{2,1,0:T(4,128)(2,1)}), bf16[16,4,256]{2,1,0:T(4,128)(2,1)S(1)}, u32[]{:S(2)}, u32[]{:S(2)}) %all-to-all-start.3) | async-done | bytes 32800 | tf_op jit(solution)/shard_map/all_to_all | solution.py:81
  58.4 3.5 all-to-all-start.1
  62.2 2.6 gather_fusion.4
  64.8 5.6 %all-to-all-done.1 = bf16[16,32,256]{2,1,0:T(8,128)(2,1)S(1)} async-done(((bf16[16,32,256]{2,1,0:T(8,128)(2,1)}), bf16[16,32,256]{2,1,0:T(8,128)(2,1)S(1)}, u32[]{:S(2)}, u32[]{:S(2)}) %all-to-all-start.1) | async-done | bytes 262176 | tf_op jit(solution)/shard_map/all_to_all | solution.py:79
  70.4 3.5 all-to-all-start.5
  74.0 18.9 %scatter_custom_fusion = f32[1835008]{0:T(1024)} fusion(s32[4096]{0:T(1024)S(1)} %bitcast.93, f32[4096]{0:T(1024)S(1)} %broadcast.222, f32[]{:T(128)} %constant.16.clone.1), kind=kCustom, calls=%fused_computation.21 | custom fusion | bytes 7340036 | tf_op jit(solution)/shard_map/scatter | solution.py:34
  92.9 9.4 %reshape.400 = f32[28,256,256]{2,1,0:T(8,128)} reshape(f32[1835008]{0:T(1024)} %scatter_custom_fusion) | data formatting | bytes 14680064 | tf_op jit(solution)/shard_map/reshape | solution.py:34
  103.1 1.2 gather_fusion.1
  104.2 1.2 gather_fusion.5
  105.4 4.5 %subtract_convert_fusion.1 = bf16[28,256,256]{2,1,0:T(8,128)(2,1)S(1)} fusion(f32[28,256,256]{2,1,0:T(8,128)} %reshape.400, f32[28,256]{1,0:T(8,128)S(1)} %convert_element_type.43, f32[256,256]{1,0:T(8,128)S(1)} %convert_element_type.41, bf16[256,256]{1,0:T(8,128)(2,1)S(1)} %gather_fusion.5), kind=kOutput, calls=%fused_computation.16 | convolution fusion | flops 952369152 | bytes 11431936 | tf_op jit(solution)/shard_map/kir,jr->kij/dot_general | solution.py:32
  109.9 2.1 multiply_reduce_fusion
  112.0 0.7 scatter_custom_fusion.5
  113.3 6.9 %all-to-all-start.8 = ((f32[16,4,256]{2,1,0:T(4,128)}), f32[16,4,256]{2,1,0:T(4,128)S(1)}, u32[]{:S(2)}, u32[]{:S(2)}) async-start(f32[16,4,256]{2,1,0:T(4,128)} %reshape.407), calls=%async_computation.8 | async-start | bytes 131072 | tf_op jit(solution)/shard_map/all_to_all | solution.py:93
  120.2 4.0 %fusion.8 = f32[256,256]{1,0:T(8,128)} fusion(bf16[28,256,256]{2,1,0:T(8,128)(2,1)} %copy-done.3, f32[28,256]{1,0:T(8,128)S(1)} %convert_element_type.43, f32[256,256]{1,0:T(8,128)S(1)} %convert_element_type.41), kind=kOutput, calls=%fused_computation.28 | convolution fusion | flops 943194112 | bytes 4222976 | tf_op jit(solution)/shard_map/kij,kir->jr/dot_general | solution.py:39
  124.2 2.6 scatter_custom_fusion.3
  126.8 0.9 all-to-all-done.8
  127.7 6.0 %all-to-all-start.7 = ((f32[16,32,256]{2,1,0:T(8,128)}), f32[16,32,256]{2,1,0:T(8,128)}, u32[]{:S(2)}, u32[]{:S(2)}) async-start(f32[16,32,256]{2,1,0:T(8,128)} %bitcast.33), calls=%async_computation.7 | async-start | bytes 1048576 | tf_op jit(solution)/shard_map/all_to_all | solution.py:92
  133.8 11.6 %subtract_convert_fusion = bf16[4096,2048]{1,0:T(8,128)(2,1)} fusion(bf16[4096,2048]{1,0:T(8,128)(2,1)} %param.15, bf16[4096,256]{1,0:T(8,128)(2,1)S(1)} %copy-done, bf16[2048,256]{1,0:T(8,128)(2,1)S(1)} %copy-done.2), kind=kOutput, calls=%fused_computation.13 | convolution fusion | flops 4320133120 | bytes 36700160 | tf_op jit(solution)/shard_map/dot_general | solution.py:104
  145.3 2.6 scatter_custom_fusion.1
  147.9 6.9 %all-to-all-start.6 = ((f32[16,32,256]{2,1,0:T(8,128)}), f32[16,32,256]{2,1,0:T(8,128)S(1)}, u32[]{:S(2)}, u32[]{:S(2)}) async-start(f32[16,32,256]{2,1,0:T(8,128)} %bitcast.29), calls=%async_computation.6 | async-start | bytes 1048576 | tf_op jit(solution)/shard_map/all_to_all | solution.py:91
  154.8 12.5 %convolution_multiply_fusion = f32[4096,256]{1,0:T(8,128)} fusion(bf16[4096,2048]{1,0:T(8,128)(2,1)} %subtract_convert_fusion, bf16[2048,256]{1,0:T(8,128)(2,1)} %param.16), kind=kOutput, calls=%fused_computation.18 | convolution fusion | flops 4296015872 | bytes 22020096 | tf_op jit(solution)/shard_map/dot_general | solution.py:108
  167.9 0.7 reduce.17
  168.7 0.7 reduce.15
  169.4 0.7 reduce.16
  170.2 1.5 scatter_custom_fusion.6
  171.7 5.2 %scatter_custom_fusion.4 = f32[2048,256]{1,0:T(8,128)} fusion(s32[512]{0:T(512)S(1)} %bitcast.106, f32[512,256]{1,0:T(8,128)} %bitcast.34, f32[]{:T(128)} %constant.16.clone.1), kind=kCustom, calls=%fused_computation.29 | custom fusion | flops 131072 | bytes 2097664 | tf_op jit(solution)/shard_map/scatter-add | solution.py:102
  176.9 7.1 %scatter_fusion = f32[4096,256]{1,0:T(8,128)} fusion(f32[4096,256]{1,0:T(8,128)} %convolution_multiply_fusion, s32[512]{0:T(512)S(1)} %bitcast.94, f32[512,256]{1,0:T(8,128)S(1)} %bitcast.88), kind=kCustom, calls=%fused_computation.8 | custom fusion | flops 131072 | bytes 1574912 | tf_op jit(solution)/shard_map/scatter-add | solution.py:99
  184.1 9.8 %convolution_multiply_fusion.1 = f32[2048,256]{1,0:T(8,128)} fusion(bf16[4096,2048]{1,0:T(8,128)(2,1)} %subtract_convert_fusion, bf16[4096,256]{1,0:T(8,128)(2,1)S(1)} %copy-done), kind=kOutput, calls=%fused_computation.27 | convolution fusion | flops 4295491584 | bytes 20971520 | tf_op jit(solution)/shard_map/dot_general | solution.py:109
  194.0 23.9 %all-reduce.6.cloned.1.call-done = (f32[4096,256]{1,0:T(8,128)}, f32[2048,256]{1,0:T(8,128)}, f32[64,256]{1,0:T(8,128)}) async-done(((f32[4096,256]{1,0:T(8,128)}, f32[2048,256]{1,0:T(8,128)}, f32[64,256]{1,0:T(8,128)}), (f32[4096,256]{1,0:T(8,128)}, f32[2048,256]{1,0:T(8,128)}, f32[64,256]{1,0:T(8,128)})) %all-reduce.6.cloned.1.call-update) | async-done | bytes 6357008 | tf_op jit(solution)/shard_map/psum | solution.py:113
  217.9 1.4 constant_dynamic-slice_fusion
  219.3 2.3 constant_dynamic-slice_fusion.1
  221.5 3.0 constant_dynamic-slice_fusion.2
  224.6 125.9 %all-reduce.4.cloned.1.call-done = f32[2048,256]{1,0:T(8,128)} async-done(((f32[2048,256]{1,0:T(8,128)}), f32[2048,256]{1,0:T(8,128)}) %all-reduce.4.cloned.1.call-update) | async-done | bytes 2097168 | tf_op jit(solution)/shard_map/psum | solution.py:112
  350.5 3.0 copy.48
  (63 shorter events, 6.3 us)
Async XLA Ops:
  7.2 43.9 %copy-start = (bf16[4096,256]{1,0:T(8,128)(2,1)S(1)}, bf16[4096,256]{1,0:T(8,128)(2,1)}, u32[]{:S(2)}) copy-start(bf16[4096,256]{1,0:T(8,128)(2,1)} %param.12) | copy-start | bytes 6291460
  7.2 55.1 %copy-start.1 = (bf16[2048,256]{1,0:T(8,128)(2,1)S(1)}, bf16[2048,256]{1,0:T(8,128)(2,1)}, u32[]{:S(2)}) copy-start(bf16[2048,256]{1,0:T(8,128)(2,1)} %param.13) | copy-start | bytes 3145732
  8.7 15.5 %all-to-all-start.2 = ((s32[16,1,4]{2,1,0:T(1,128)}), s32[16,1,4]{2,1,0:T(1,128)S(1)}, u32[]{:S(2)}, u32[]{:S(2)}) async-start(s32[16,1,4]{2,1,0:T(1,128)} %copy.36), calls=%async_computation.2 | async-start | bytes 16384 | tf_op jit(solution)/shard_map/all_to_all | solution.py:76
  24.2 12.7 %all-to-all-start = ((s32[16,1,32]{2,1,0:T(1,128)}), s32[16,1,32]{2,1,0:T(1,128)S(1)}, u32[]{:S(2)}, u32[]{:S(2)}) async-start(s32[16,1,32]{2,1,0:T(1,128)} %bitcast.95), calls=%async_computation | async-start | bytes 16384 | tf_op jit(solution)/shard_map/all_to_all | solution.py:74
  36.9 10.6 %all-to-all-start.4 = ((s32[16,1,32]{2,1,0:T(1,128)}), s32[16,1,32]{2,1,0:T(1,128)S(1)}, u32[]{:S(2)}, u32[]{:S(2)}) async-start(s32[16,1,32]{2,1,0:T(1,128)} %bitcast.96), calls=%async_computation.4 | async-start | bytes 16384 | tf_op jit(solution)/shard_map/all_to_all | solution.py:75
  47.5 10.9 %all-to-all-start.3 = ((bf16[16,4,256]{2,1,0:T(4,128)(2,1)}), bf16[16,4,256]{2,1,0:T(4,128)(2,1)S(1)}, u32[]{:S(2)}, u32[]{:S(2)}) async-start(bf16[16,4,256]{2,1,0:T(4,128)(2,1)} %reshape.426), calls=%async_computation.3 | async-start | bytes 65536 | tf_op jit(solution)/shard_map/all_to_all | solution.py:81
  58.4 12.0 %all-to-all-start.1 = ((bf16[16,32,256]{2,1,0:T(8,128)(2,1)}), bf16[16,32,256]{2,1,0:T(8,128)(2,1)S(1)}, u32[]{:S(2)}, u32[]{:S(2)}) async-start(bf16[16,32,256]{2,1,0:T(8,128)(2,1)} %bitcast.90), calls=%async_computation.1 | async-start | bytes 524288 | tf_op jit(solution)/shard_map/all_to_all | solution.py:79
  70.4 33.8 %all-to-all-start.5 = ((bf16[16,32,256]{2,1,0:T(8,128)(2,1)}), bf16[16,32,256]{2,1,0:T(8,128)(2,1)S(1)}, u32[]{:S(2)}, u32[]{:S(2)}) async-start(bf16[16,32,256]{2,1,0:T(8,128)(2,1)} %bitcast.89), calls=%async_computation.5 | async-start | bytes 524288 | tf_op jit(solution)/shard_map/all_to_all | solution.py:80
  109.9 2.1 copy-start.3
  113.3 14.4 %all-to-all-start.8 = ((f32[16,4,256]{2,1,0:T(4,128)}), f32[16,4,256]{2,1,0:T(4,128)S(1)}, u32[]{:S(2)}, u32[]{:S(2)}) async-start(f32[16,4,256]{2,1,0:T(4,128)} %reshape.407), calls=%async_computation.8 | async-start | bytes 131072 | tf_op jit(solution)/shard_map/all_to_all | solution.py:93
  120.2 13.6 %copy-start.2 = (bf16[2048,256]{1,0:T(8,128)(2,1)S(1)}, bf16[2048,256]{1,0:T(8,128)(2,1)}, u32[]{:S(2)}) copy-start(bf16[2048,256]{1,0:T(8,128)(2,1)} %param.16) | copy-start | bytes 3145732
  127.7 20.2 %all-to-all-start.7 = ((f32[16,32,256]{2,1,0:T(8,128)}), f32[16,32,256]{2,1,0:T(8,128)}, u32[]{:S(2)}, u32[]{:S(2)}) async-start(f32[16,32,256]{2,1,0:T(8,128)} %bitcast.33), calls=%async_computation.7 | async-start | bytes 1048576 | tf_op jit(solution)/shard_map/all_to_all | solution.py:92
  147.9 29.0 %all-to-all-start.6 = ((f32[16,32,256]{2,1,0:T(8,128)}), f32[16,32,256]{2,1,0:T(8,128)S(1)}, u32[]{:S(2)}, u32[]{:S(2)}) async-start(f32[16,32,256]{2,1,0:T(8,128)} %bitcast.29), calls=%async_computation.6 | async-start | bytes 1048576 | tf_op jit(solution)/shard_map/all_to_all | solution.py:91
  154.8 63.1 %all-reduce.6.cloned.1.call-start = ((), (), s32[]{:S(2)}) async-start(), calls=%async_computation.10 | async-start | bytes 12713984 | tf_op jit(solution)/shard_map/psum | solution.py:113
  184.1 166.4 %all-reduce.4.cloned.1.call-start = ((), (), s32[]{:S(2)}) async-start(), calls=%async_computation.9 | async-start | bytes 4194304 | tf_op jit(solution)/shard_map/psum | solution.py:112
Sparse Core Ops, SparseCore 0:
  184.2 33.6 all-reduce.5
  223.4 127.0 all-reduce.3
where the time goes:
time: 362 us; the launch traced here: 360 us
  waiting for transfers between devices  175 us (48%)
  local copies, waits for them, and re-layouts  59.7 us (16%)
  starting transfers between devices  47.7 us (13%)
  matrix products  44.4 us (12%)
  other arithmetic  19.7 us (5%)
  between operations  14.3 us (4%)
    psum x1, waiting for transfers between devices, local(): grad_features = lax.psum(feat_terms, 'wide')  126 us
    psum x1, waiting for transfers between devices, local(): total_u, total_v, total_w = lax.psum((dense_u, dense_v, dense_w), 'narrow')  23.9 us
    scatter x1, local copies, waits for them, and re-layouts, block_grads(): jnp.zeros((cells,), jnp.float32).at[pos].set(1.0)  18.9 us
    dot_general x1, matrix products, local(): jnp.dot(resid, feature_table, preferred_element_type=jnp.float32)  12.5 us
    dot_general x1, matrix products, local(): lax.dot_general(user_table, feature_table, (((1,), (1,)), ((), ())), pref...  11.6 us
    dot_general x1, matrix products, local(): lax.dot_general(resid, user_table, (((0,), (0,)), ((), ())), preferred_el...  9.78 us
    reshape x1, local copies, waits for them, and re-layouts, block_grads(): jnp.zeros((cells,), jnp.float32).at[pos].set(1.0)  9.43 us
    all_to_all x1, starting transfers between devices, local(): lax.all_to_all(week_need, 'wide', split_axis=0, concat_axis=0, tiled=True)  8.31 us
  transfers between devices with their start and end apart: 11, of which 8 were waited for; matrix products, arithmetic and copies ran while one was open for 29% of the time, Pallas kernels for 0%

commit v1 on v0

v1 whole, which is shorter than its diff:
```python
import functools

import jax
import jax.numpy as jnp
from jax import lax
from jax.experimental import pallas as pl
from jax.experimental.pallas import tpu as pltpu
from jax.sharding import PartitionSpec as P

RANK = 256
BU = 256
BI = 256
BW = 28
BWP = 32
CAPU = 32
CAPI = 32
CAPW = 4
SLOT = 80
TAIL = 16
HALF = 14
F32, BF16, I32, I16 = jnp.float32, jnp.bfloat16, jnp.int32, jnp.int16
NN = (((1,), (0,)), ((), ()))
NT = (((1,), (1,)), ((), ()))
TN = (((0,), (0,)), ((), ()))


def mm(a, b, dims=NN):
    return lax.dot_general(a, b, dims, preferred_element_type=F32)


def iota(shape, dim):
    return lax.broadcasted_iota(I32, shape, dim)


def params(**kw):
    return pltpu.CompilerParams(vmem_limit_bytes=56 << 20, **kw)


def cost(flops, nbytes):
    return pl.CostEstimate(flops=flops, bytes_accessed=nbytes, transcendentals=0)


VM = pl.BlockSpec(memory_space=pltpu.VMEM)
SM = pl.BlockSpec(memory_space=pltpu.SMEM)


def pow2(e):
    return jnp.exp2(e).astype(BF16).astype(F32)


def row_exponent(g):
    m = jnp.max(jnp.abs(g), axis=1, keepdims=True)
    return jnp.clip(jnp.ceil(jnp.log2(jnp.maximum(m, 1e-30))), -96.0, 110.0)


def column_of(row):
    return jnp.broadcast_to(row, (128, 128)).T[:, :1]


def gather_kernel(owners, got_ref, ut_ref, it_ref, wt_ref, out_ref):
    got = got_ref[...]
    flip = jnp.concatenate([got, jnp.zeros((128 - owners, 128), I32)], axis=0).T

    def pick(first, count, table_ref, step):
        col = jnp.concatenate([flip[first : first + count, w : w + 1] for w in range(owners)], axis=0)
        rows = table_ref.shape[0]
        acc = None
        for c in range(0, rows, step):
            hit = iota((owners * count, step), 1) == col - c
            part = mm(jnp.where(hit, 1.0, 0.0).astype(BF16), table_ref[c : c + step, :])
            acc = part if acc is None else acc + part
        return acc.astype(BF16)

    u = pick(0, CAPU, ut_ref, 512)
    v = pick(CAPU, CAPI, it_ref, 512)
    w = pick(CAPU + CAPI, TAIL, wt_ref, wt_ref.shape[0])
    for o in range(owners):
        b = SLOT * o
        out_ref[b : b + CAPU, :] = u[CAPU * o : CAPU * (o + 1)]
        out_ref[b + CAPU : b + CAPU + CAPI, :] = v[CAPI * o : CAPI * (o + 1)]
        out_ref[b + CAPU + CAPI : b + SLOT, :] = w[TAIL * o : TAIL * (o + 1)]


def gather_rows(got, ut, it, wt):
    owners = got.shape[0]
    return pl.pallas_call(
        functools.partial(gather_kernel, owners),
        in_specs=[VM] * 4,
        out_specs=VM,
        out_shape=jax.ShapeDtypeStruct((owners * SLOT, RANK), BF16),
        compiler_params=params(),
        cost_estimate=cost(2 << 30, 4 << 20),
        name="gather_rows",
    )(got, ut, it, wt)


def positives_kernel(p_ref, out_ref):
    n = p_ref.shape[0]
    rows = [p_ref[c : c + 1, :] for c in range(n)]
    near = [None] * n
    for a in range(n):
        col = jnp.broadcast_to(rows[a], (128, 128)).T
        for c in range(a, n):
            x = col ^ rows[c]
            if c == a:
                x = jnp.where(iota((128, 128), 0) < iota((128, 128), 1), x, 1)
            best = x[0:8]
            for s in range(8, 128, 8):
                best = jnp.minimum(best, x[s : s + 8])
            near[c] = best if near[c] is None else jnp.minimum(near[c], best)
    lo = hi = None
    group = 4
    for g in range(0, n, group):
        pos = jnp.concatenate(rows[g : g + group], axis=1)
        first = jnp.concatenate([jnp.min(near[c], axis=0, keepdims=True) for c in range(g, g + group)], axis=1)
        week = pos >> 16
        bit = jnp.where(first == 0, 0, 1)
        low = jnp.where(week < HALF, bit << week, 0).astype(F32)
        high = jnp.where(week < HALF, 0, bit << jnp.maximum(week - HALF, 0)).astype(F32)
        user_hit = iota((BU, group * 128), 0) == (pos >> 8) & (BU - 1)
        item_hit = iota((BI, group * 128), 0) == pos & (BI - 1)
        item = jnp.where(item_hit, 1.0, 0.0).astype(BF16)
        part_lo = mm(jnp.where(user_hit, low, 0.0).astype(BF16), item, NT)
        part_hi = mm(jnp.where(user_hit, high, 0.0).astype(BF16), item, NT)
        lo = part_lo if lo is None else lo + part_lo
        hi = part_hi if hi is None else hi + part_hi
    out_ref[...] = lo.astype(I32) | (hi.astype(I32) << HALF)


def positives(pos):
    return pl.pallas_call(
        positives_kernel,
        in_specs=[VM],
        out_specs=VM,
        out_shape=jax.ShapeDtypeStruct((BU, BI), I32),
        compiler_params=params(),
        cost_estimate=cost(4 << 30, 1 << 20),
        name="positives",
    )(pos.reshape(-1, 128))


def block_kernel(owners, back_ref, bits_ref, uc_ref, vc_ref, wc_ref, out_ref, gu, gvt, gw):
    def listed(count_ref, cap, stride, first, total):
        slots = owners * stride
        lane = iota((1, slots), 1)
        place = jnp.full((1, slots), -1, I32)
        start = 0
        back = []
        for o in range(owners):
            n = count_ref[0, o]
            s = lane - stride * o
            place = jnp.where((s >= 0) & (s < n), start + s, place)
            sub = iota((stride, total), 0)
            hit = (iota((stride, total), 1) == sub + start) & (sub < n)
            back.append(jnp.where(hit, 1.0, 0.0))
            start = start + n
        hit = iota((total, slots), 0) == place
        got = jnp.concatenate(
            [back_ref[SLOT * o + first : SLOT * o + first + stride, :] for o in range(owners)], axis=0
        )
        rows = mm(jnp.where(hit, 1.0, 0.0).astype(BF16), got)
        return rows, hit, jnp.concatenate(back, axis=0).astype(BF16)

    u, hit_u, into_u = listed(uc_ref, CAPU, CAPU, 0, BU)
    v, hit_v, into_v = listed(vc_ref, CAPI, CAPI, CAPU, BI)
    w, hit_w, into_w = listed(wc_ref, CAPW, TAIL, CAPU + CAPI, BWP)
    vb = v.astype(BF16)
    ut = u.T
    wt = jnp.concatenate([w, jnp.zeros((128 - BWP, RANK), F32)], axis=0).T
    gw[...] = jnp.zeros_like(gw)
    bits = bits_ref
    for k in range(BW):
        wk = w[k : k + 1, :]
        uw = (u * wk).astype(BF16)
        m = mm(uw, vb, NT)
        pos = ((bits[...] >> k) & 1).astype(F32)
        g = (1.0 / (1.0 + jnp.exp(-m)) - pos).astype(BF16)
        q = mm(g, vb)
        uwt = (ut * wt[:, k : k + 1]).astype(BF16)
        pv = mm(uwt, g)
        if k == 0:
            gu[...] = q * wk
            gvt[...] = pv
        else:
            gu[...] += q * wk
            gvt[...] += pv
        gw[k : k + 1, :] = jnp.sum(q * u, axis=0, keepdims=True)

    def slots_of(g, hit, into):
        e = row_exponent(g)
        q = jnp.round(g * pow2(14.0 - e))
        hi = jnp.round(q * (1.0 / 256.0))
        lo = q - 256.0 * hi
        placed = 256.0 * mm(into, hi.astype(BF16)) + mm(into, lo.astype(BF16))
        row = jnp.sum(jnp.where(hit, e, 0.0), axis=0, keepdims=True)
        return placed, row

    qu, eu = slots_of(gu[...], hit_u, into_u)
    qv, ev = slots_of(gvt[...].T, hit_v, into_v)
    qw, ew = slots_of(gw[...], hit_w, into_w)
    lane = iota((8, 128), 1)

    def to_lane(row, width, o, lane_at):
        per = 128 // width
        cut = jnp.broadcast_to(row[:, 128 * (o // per) : 128 * (o // per + 1)], (8, 128))
        return pltpu.roll(cut, (lane_at - width * (o % per)) % 128, 1)

    sub = iota((TAIL, RANK), 0)
    for o in range(owners):
        b = SLOT * o
        out_ref[b : b + CAPU, :] = qu[CAPU * o : CAPU * (o + 1)].astype(I32).astype(I16)
        out_ref[b + CAPU : b + CAPU + CAPI, :] = qv[CAPI * o : CAPI * (o + 1)].astype(I32).astype(I16)
        exps = jnp.where(
            lane < CAPU,
            to_lane(eu, CAPU, o, 0),
            jnp.where(lane < CAPU + CAPI, to_lane(ev, CAPI, o, CAPU), to_lane(ew, TAIL, o, CAPU + CAPI)),
        )
        exps = jnp.concatenate([exps[0:1], exps[0:1]], axis=1)
        tail = jnp.where(sub == 8, exps, jnp.where(sub < CAPW, qw[TAIL * o : TAIL * (o + 1)], 0.0))
        out_ref[b + CAPU + CAPI : b + SLOT, :] = tail.astype(I32).astype(I16)


def block_slots(back, bits, uc, vc, wc):
    owners = uc.shape[1]
    return pl.pallas_call(
        functools.partial(block_kernel, owners),
        in_specs=[VM, VM, SM, SM, SM],
        out_specs=VM,
        out_shape=jax.ShapeDtypeStruct((owners * SLOT, RANK), I16),
        scratch_shapes=[pltpu.VMEM((BU, RANK), F32), pltpu.VMEM((RANK, BI), F32), pltpu.VMEM((BWP, RANK), F32)],
        compiler_params=params(),
        cost_estimate=cost(4 << 30, 2 << 20),
        name="block_slots",
    )(back, bits, uc, vc, wc)


def dense_kernel(shares, per, chunk, n_ref, x_ref, u_ref, f_ref, others_ref, mine_ref, gf_ref, acc):
    t = pl.program_id(0)
    u = u_ref[...]
    nf = f_ref.shape[0]

    @pl.when(t == 0)
    def _():
        acc[...] = jnp.zeros_like(acc)

    total = None
    for c in range(0, nf, chunk):
        f = f_ref[c : c + chunk, :]
        r = (mm(u, f, NT) - x_ref[:, c : c + chunk].astype(F32)).astype(BF16)
        part = mm(r, f)
        total = part if total is None else total + part
        acc[c : c + chunk, :] += mm(r, u, TN)

    @pl.when(t < (shares - 1) * per)
    def _():
        others_ref[...] = 0.0625 * total

    @pl.when(t >= (shares - 1) * per)
    def _():
        mine_ref[...] = 0.0625 * total

    @pl.when(t == pl.num_programs(0) - 1)
    def _():
        pack_features(0.0625 * acc[...], gf_ref)


def pack_features(g, out_ref):
    nf = g.shape[0]
    c = nf // 16
    eye = iota((c, 128), 0) == iota((c, 128), 1)
    for o in range(16):
        part = g[c * o : c * (o + 1)]
        e = row_exponent(part)
        q = jnp.round(part * pow2(14.0 - e))
        row = jnp.sum(jnp.where(eye, e, 0.0), axis=0, keepdims=True)
        row = jnp.concatenate([row, row], axis=1)
        b = (c + TAIL) * o
        out_ref[b : b + c, :] = q.astype(I32).astype(I16)
        tail = jnp.where(iota((TAIL, RANK), 0) == 8, row, 0.0)
        out_ref[b + c : b + c + TAIL, :] = tail.astype(I32).astype(I16)


def dense(n, x, u, f, shares):
    nu, nf = x.shape
    own = nu // shares
    tile = 512
    per = own // tile
    tiles = nu // tile

    def rows(t, n_ref):
        return (lax.rem(n_ref[0] + 1 + t // per, shares) * per + lax.rem(t, per), 0)

    return pl.pallas_call(
        functools.partial(dense_kernel, shares, per, nf),
        grid_spec=pltpu.PrefetchScalarGridSpec(
            num_scalar_prefetch=1,
            grid=(tiles,),
            in_specs=[
                pl.BlockSpec((tile, nf), rows),
                pl.BlockSpec((tile, RANK), rows),
                pl.BlockSpec((nf, RANK), lambda t, n_ref: (0, 0)),
            ],
            out_specs=[
                pl.BlockSpec((tile, RANK), lambda t, n_ref: (jnp.minimum(t, (shares - 1) * per - 1), 0)),
                pl.BlockSpec((tile, RANK), lambda t, n_ref: (jnp.maximum(t - (shares - 1) * per, 0), 0)),
                pl.BlockSpec((nf + 16 * TAIL, RANK), lambda t, n_ref: (0, 0)),
            ],
            scratch_shapes=[pltpu.VMEM((nf, RANK), F32)],
        ),
        out_shape=[
            jax.ShapeDtypeStruct(((shares - 1) * own, RANK), F32),
            jax.ShapeDtypeStruct((own, RANK), F32),
            jax.ShapeDtypeStruct((nf + 16 * TAIL, RANK), I16),
        ],
        compiler_params=params(dimension_semantics=("arbitrary",)),
        cost_estimate=cost(3 * 2 * nu * nf * RANK, 2 * nu * nf + 8 * nu * RANK),
        name="dense",
    )(n, x, u, f)


def unpacked(block, c):
    q = block[:c].astype(I32).astype(F32)
    e = block[c : c + TAIL].astype(I32).astype(F32)[8:9, :128]
    return q * pow2(column_of(e)[:c] - 14.0)


def sum_kernel(c, in_ref, a_ref, b_ref):
    total = None
    for o in range(16):
        part = unpacked(in_ref[(c + TAIL) * o : (c + TAIL) * (o + 1), :], c)
        total = part if total is None else total + part
    e = row_exponent(total)
    q = jnp.round(total * pow2(14.0 - e)).astype(I32)
    eye = iota((c, 128), 0) == iota((c, 128), 1)
    row = jnp.sum(jnp.where(eye, e, 0.0), axis=0, keepdims=True)
    tail = jnp.where(iota((TAIL, 128), 0) == 8, row, 0.0)
    a_ref[:c, :] = q[:, :128].astype(I16)
    a_ref[c:, :] = tail.astype(I32).astype(I16)
    b_ref[...] = q[:, 128:].astype(I16)


def sum_features(parts, c):
    return pl.pallas_call(
        functools.partial(sum_kernel, c),
        in_specs=[VM],
        out_specs=[VM, VM],
        out_shape=[jax.ShapeDtypeStruct((c + TAIL, 128), I16), jax.ShapeDtypeStruct((c, 128), I16)],
        compiler_params=params(),
        cost_estimate=cost(1 << 20, 2 << 20),
        name="sum_features",
    )(parts)


ORDER_A = (8, 4, 2, 1)
ORDER_B = (8, 4, 1, 2)


def spread(x, order):
    for bit in order:
        x = jnp.concatenate([x, lax.ppermute(x, "wide", [(i, i ^ bit) for i in range(16)])], axis=0)
    return x


def flips(order):
    out = []
    for j in range(16):
        out.append(sum(bit for i, bit in enumerate(order) if (j >> i) & 1))
    return out


def decode_kernel(c, w_ref, a_ref, b_ref, out_ref):
    me = w_ref[0]
    at_b = flips(ORDER_B)
    for j, flip in enumerate(flips(ORDER_A)):
        i = at_b.index(flip)
        base = (c + TAIL) * j
        e = a_ref[base + c : base + c + TAIL, :].astype(I32).astype(F32)[8:9, :]
        scale = pow2(column_of(e)[:c] - 14.0)
        at = pl.multiple_of((me ^ flip) * c, c)
        out_ref[pl.ds(at, c), :128] = a_ref[base : base + c, :].astype(I32).astype(F32) * scale
        out_ref[pl.ds(at, c), 128:] = b_ref[c * i : c * (i + 1), :].astype(I32).astype(F32) * scale


def decode_features(w, a, b, c):
    return pl.pallas_call(
        functools.partial(decode_kernel, c),
        in_specs=[SM, VM, VM],
        out_specs=VM,
        out_shape=jax.ShapeDtypeStruct((16 * c, RANK), F32),
        compiler_params=params(),
        cost_estimate=cost(1 << 20, 3 << 20),
        name="decode_features",
    )(w, a, b)


def lanes(x, width, off):
    per = 128 // width
    rolled = [pltpu.roll(x, (width * j - off) % 128, 1) for j in range(per)]
    lane = iota((1, 128), 1) // width
    out = []
    for g in range(16 // per):
        acc = rolled[0][per * g : per * g + 1, :]
        for j in range(1, per):
            acc = jnp.where(lane == j, rolled[j][per * g + j : per * g + j + 1, :], acc)
        out.append(acc)
    return jnp.concatenate(out, axis=1)


def owner_kernel(shares, n_ref, *refs):
    gots, rets = refs[:shares], refs[shares : 2 * shares]
    parts = refs[2 * shares : 3 * shares]
    users_ref, items_ref, weeks_ref = refs[3 * shares :]
    n = n_ref[0]
    kinds = []
    for got_ref, ret_ref in zip(gots, rets):
        got = got_ref[...]
        tails = [
            ret_ref[SLOT * o + CAPU + CAPI : SLOT * (o + 1), :].astype(I32).astype(F32) for o in range(16)
        ]
        exps = jnp.concatenate([t[8:9, :128] for t in tails], axis=0)
        scale = pow2(exps - 14.0)

        def split(q):
            hi = jnp.round(q * (1.0 / 256.0))
            return hi.astype(BF16), (q - 256.0 * hi).astype(BF16)

        def rows(first, count):
            return jnp.concatenate(
                [ret_ref[SLOT * o + first : SLOT * o + first + count, :] for o in range(16)], axis=0
            ).astype(I32).astype(F32)

        tail_ok = iota((1, 16 * TAIL), 1) % TAIL < CAPW
        wk = jnp.where(tail_ok, lanes(got, TAIL, CAPU + CAPI), -1)
        kinds.append(
            (
                (lanes(got, CAPU, 0), lanes(scale, CAPU, 0), split(rows(0, CAPU))),
                (lanes(got, CAPI, CAPU), lanes(scale, CAPI, CAPU), split(rows(CAPU, CAPI))),
                (wk, lanes(scale, TAIL, CAPU + CAPI), split(jnp.concatenate(tails, axis=0))),
            )
        )

    def scatter(kind, base, size):
        total = None
        for source in kinds:
            req, scale, (hi, lo) = source[kind]
            hit = iota((size, req.shape[1]), 0) + base == req
            put = jnp.where(hit, scale, 0.0).astype(BF16)
            part = 256.0 * mm(put, hi) + mm(put, lo)
            total = part if total is None else total + part
        return total

    own_u, own_i, own_w = users_ref.shape[0], items_ref.shape[0], weeks_ref.shape[0]
    step = min(512, own_u)
    for c in range(0, own_u, step):
        dense_part = parts[0][c : c + step, :]
        for p in parts[1:]:
            dense_part = dense_part + p[c : c + step, :]
        users_ref[c : c + step, :] = dense_part + scatter(0, n * own_u + c, step)
    step = min(512, own_i)
    for c in range(0, own_i, step):
        items_ref[c : c + step, :] = scatter(1, n * own_i + c, step)
    weeks_ref[...] = scatter(2, n * own_w, own_w)


def owner_sums(n, gots, rets, parts, own_u, own_i, own_w):
    shares = len(gots)
    return pl.pallas_call(
        functools.partial(owner_kernel, shares),
        in_specs=[SM] + [VM] * (3 * shares),
        out_specs=[VM] * 3,
        out_shape=[jax.ShapeDtypeStruct((r, RANK), F32) for r in (own_u, own_i, own_w)],
        compiler_params=params(),
        cost_estimate=cost(6 << 30, 8 << 20),
        name="owner_sums",
    )(n, *gots, *rets, *parts)


def local(
    user_table,
    item_table,
    week_table,
    profile,
    feature_table,
    user_req,
    item_req,
    week_req,
    user_counts,
    item_counts,
    week_counts,
    pos_cells,
):
    owners = lax.axis_size("wide")
    shares = lax.axis_size("narrow")
    n = lax.axis_index("narrow").astype(I32).reshape(1)
    w = lax.axis_index("wide").astype(I32).reshape(1)

    def across(x):
        return lax.all_to_all(x, "wide", split_axis=0, concat_axis=0, tiled=True)

    def shift(x, r):
        return lax.ppermute(x, "narrow", [(i, (i + r) % shares) for i in range(shares)])

    spare = jnp.zeros((owners, 128 - CAPU - CAPI - CAPW), I32)
    got = across(jnp.concatenate([user_req[0], item_req[0], week_req[0], spare], axis=1))
    back = across(gather_rows(got, user_table, item_table, week_table))
    bits = positives(pos_cells[0])
    others, mine, packed = dense(n, profile, user_table, feature_table, shares)
    own_u = mine.shape[0]
    c = feature_table.shape[0] // 16
    shard_a, shard_b = sum_features(across(packed), c)
    grad_features = decode_features(w, spread(shard_a, ORDER_A), spread(shard_b, ORDER_B), c)
    ret = across(block_slots(back, bits, user_counts, item_counts, week_counts))
    gots = [got] + [shift(got, r) for r in range(1, shares)]
    rets = [ret] + [shift(ret, r) for r in range(1, shares)]
    parts = [mine] + [shift(others[own_u * (r - 1) : own_u * r], r) for r in range(1, shares)]
    grad_users, grad_items, grad_weeks = owner_sums(
        n, gots, rets, parts, own_u, item_table.shape[0] // shares, week_table.shape[0] // shares
    )
    return (grad_users, grad_items, grad_weeks, grad_features)


def solution(mesh):
    return jax.shard_map(
        local,
        mesh=mesh,
        in_specs=(
            P("wide", None),
            P("wide", None),
            P("wide", None),
            P("wide", "narrow"),
            P("narrow", None),
            P(("wide", "narrow"), None, None),
            P(("wide", "narrow"), None, None),
            P(("wide", "narrow"), None, None),
            P(("wide", "narrow"), None),
            P(("wide", "narrow"), None),
            P(("wide", "narrow"), None),
            P(("wide", "narrow"), None),
        ),
        out_specs=(
            P(("wide", "narrow"), None),
            P(("wide", "narrow"), None),
            P(("wide", "narrow"), None),
            P("narrow", None),
        ),
        check_vma=False,
    )
```

time: 362 us -> 140 us (0.39)
  waiting for transfers between devices: 175 us -> 33.6 us
  local copies, waits for them, and re-layouts: 59.7 us -> 4.21 us
  Pallas kernels: 0 us -> 51.9 us
  matrix products: 44.4 us -> 0 us
  starting transfers between devices: 47.7 us -> 27.5 us
  blocking collectives: 0 us -> 15.3 us
  other arithmetic: 19.7 us -> 5.44 us
  between operations: 14.3 us -> 0.82 us
    psum x2 -> x0, waiting for transfers between devices: 150 us -> none  [the longest x1 126 us: local(): grad_features = lax.psum(feat_terms, 'wide')]
    pallas_call x0 -> x7, Pallas kernels: none -> 51.9 us  [the longest x1 19.8 us: dense(): pl.pallas_call(functools.partial(dense_kernel, shares, per, nf), grid_spe...]
    dot_general x6 -> x0, matrix products: 44.4 us -> none  [the longest x1 12.5 us: local(): jnp.dot(resid, feature_table, preferred_element_type=jnp.float32)]
    all_to_all x9 -> x3, starting transfers between devices: 47.6 us -> 16.7 us  [across(): return lax.all_to_all(x, 'wide', split_axis=0, concat_axis=0, tiled=True)]
    scatter x4 -> x0, local copies, waits for them, and re-layouts: 24.9 us -> none  [the longest x1 18.9 us: block_grads(): jnp.zeros((cells,), jnp.float32).at[pos].set(1.0)]
    ppermute x0 -> x11, waiting for transfers between devices: none -> 23 us  [the longest x8 23 us: spread(): lax.ppermute(x, 'wide', [(i, i ^ bit) for i in range(16)])]
    all_to_all x0 -> x1, blocking collectives: none -> 15.3 us  [across(): return lax.all_to_all(x, 'wide', split_axis=0, concat_axis=0, tiled=True)]
    all_to_all x9 -> x3, waiting for transfers between devices: 24.7 us -> 10.6 us  [across(): return lax.all_to_all(x, 'wide', split_axis=0, concat_axis=0, tiled=True)]
  transfers between devices with their start and end apart: 11 -> 14, of which waited for: 8 -> 7; matrix products, arithmetic and copies ran while one was open for 29% -> 5% of each run, Pallas kernels for 0% -> 29%
where the time goes in v1:
time: 140 us; the launch traced here: 139 us
  Pallas kernels  51.9 us (37%)
  waiting for transfers between devices  33.6 us (24%)
  starting transfers between devices  27.5 us (20%)
  blocking collectives  15.3 us (11%)
  other arithmetic  5.44 us (4%)
  local copies, waits for them, and re-layouts  4.21 us (3%)
    ppermute x8, waiting for transfers between devices, spread(): lax.ppermute(x, 'wide', [(i, i ^ bit) for i in range(16)])  23 us
    pallas_call x1, Pallas kernels, dense(): pl.pallas_call(functools.partial(dense_kernel, shares, per, nf), grid_spe...  19.8 us
    all_to_all x3, starting transfers between devices, across(): return lax.all_to_all(x, 'wide', split_axis=0, concat_axis=0, tiled=True)  16.7 us
    all_to_all x1, blocking collectives, across(): return lax.all_to_all(x, 'wide', split_axis=0, concat_axis=0, tiled=True)  15.3 us
    all_to_all x3, waiting for transfers between devices, across(): return lax.all_to_all(x, 'wide', split_axis=0, concat_axis=0, tiled=True)  10.6 us
    ppermute x8, starting transfers between devices, spread(): lax.ppermute(x, 'wide', [(i, i ^ bit) for i in range(16)])  10.2 us
    pallas_call x1, Pallas kernels, block_slots(): pl.pallas_call(functools.partial(block_kernel, owners), in_specs=[VM, VM,...  8.12 us
    pallas_call x1, Pallas kernels, owner_sums(): pl.pallas_call(functools.partial(owner_kernel, shares), in_specs=[SM] + [...  7.19 us
  transfers between devices with their start and end apart: 14, of which 7 were waited for; matrix products, arithmetic and copies ran while one was open for 5% of the time, Pallas kernels for 29%

profile of v1, /device:TPU:0, one launch (start us, length us, event | category | flops | bytes accessed | tf_op | source)
XLA Modules:
  0.0 138.8 jit_solution(17474960915400017832)
XLA Ops:
  0.6 0.8 copy.17
  1.4 0.1 pad.21.clone
  1.5 0.8 add_add_fusion
  2.3 15.3 %all_to_all.44 = s32[16,1,128]{2,1,0:T(1,128)} all-to-all(s32[16,1,128]{2,1,0:T(1,128)S(1)} %bitcast.21), channel_id=1, replica_groups=mesh['wide'=16,'narrow'=2] {'wide'}, dimensions={0} | all-to-all | bytes 16384 | tf_op jit(solution)/shard_map/all_to_all | solution.py:498
  17.6 4.8 %gather_rows.1 = bf16[1280,256]{1,0:T(8,128)(2,1)} custom-call(s32[16,128]{1,0:T(8,128)} %bitcast.22, bf16[4096,256]{1,0:T(8,128)(2,1)} %u_ref.1, bf16[2048,256]{1,0:T(8,128)(2,1)} %it_ref.1, bf16[64,256]{1,0:T(8,128)(2,1)} %wt_ref.1), custom_call_target="tpu_custom_call" | custom-call | flops 2147483648 | bytes 4194304 | tf_op jit(solution)/shard_map/gather_rows/pallas_call | solution.py:86
  22.4 3.6 %all-to-all-start.1 = ((bf16[16,80,256]{2,1,0:T(8,128)(2,1)}), bf16[16,80,256]{2,1,0:T(8,128)(2,1)S(1)}, u32[]{:S(2)}, u32[]{:S(2)}) async-start(bf16[16,80,256]{2,1,0:T(8,128)(2,1)} %bitcast.20), calls=%async_computation.1 | async-start | bytes 1310720 | tf_op jit(solution)/shard_map/all_to_all | solution.py:498
  26.0 19.8 %dense.1 = (f32[2048,256]{1,0:T(8,128)}, f32[2048,256]{1,0:T(8,128)}, s16[2304,256]{1,0:T(8,128)(2,1)}) custom-call(s32[1]{0:T(128)} %bitcast.n_ref, bf16[4096,2048]{1,0:T(8,128)(2,1)} %x_ref.1, bf16[4096,256]{1,0:T(8,128)(2,1)} %u_ref.1, bf16[2048,256]{1,0:T(8,128)(2,1)} %f_ref.1), custom_call_target="tpu_custom_call" | custom-call | flops 12884901888 | bytes 25165824 | tf_op jit(solution)/shard_map/dense/pallas_call | solution.py:293
  45.9 0.0 all-to-all-done.1
  45.9 0.0 copy-start.3
  45.9 6.9 %all-to-all-start.3 = ((s16[16,144,256]{2,1,0:T(8,128)(2,1)}), s16[16,144,256]{2,1,0:T(8,128)(2,1)S(1)}, u32[]{:S(2)}, u32[]{:S(2)}) async-start(s16[16,144,256]{2,1,0:T(8,128)(2,1)} %bitcast.15), calls=%async_computation.3 | async-start | bytes 2359296 | tf_op jit(solution)/shard_map/all_to_all | solution.py:498
  52.8 0.1 collective-permute-start.2
  52.9 6.1 %positives.1.bits_ref = s32[256,256]{1,0:T(8,128)} custom-call(s32[32,128]{1,0:T(8,128)} %bitcast.28), custom_call_target="tpu_custom_call" | custom-call | flops 4294967296 | bytes 1048576 | tf_op jit(solution)/shard_map/positives/pallas_call | solution.py:131
  59.0 0.5 collective-permute-start
  59.5 8.1 %block_slots.1 = s16[1280,256]{1,0:T(8,128)(2,1)} custom-call(bf16[1280,256]{1,0:T(8,128)(2,1)} %bitcast.19, s32[256,256]{1,0:T(8,128)} %positives.1.bits_ref, s32[1,16]{1,0:T(1,128)} %uc_ref.1, s32[1,16]{1,0:T(1,128)} %vc_ref.1, s32[1,16]{1,0:T(1,128)} %wc_ref.1), custom_call_target="tpu_custom_call" | custom-call | flops 4294967296 | bytes 2097152 | tf_op jit(solution)/shard_map/block_slots/pallas_call | solution.py:225
  67.6 10.6 %all-to-all-done.3 = s16[16,144,256]{2,1,0:T(8,128)(2,1)S(1)} async-done(((s16[16,144,256]{2,1,0:T(8,128)(2,1)}), s16[16,144,256]{2,1,0:T(8,128)(2,1)S(1)}, u32[]{:S(2)}, u32[]{:S(2)}) %all-to-all-start.3) | async-done | bytes 1179680 | tf_op jit(solution)/shard_map/all_to_all | solution.py:498
  78.2 6.2 %all-to-all-start.2 = ((s16[16,80,256]{2,1,0:T(8,128)(2,1)}), s16[16,80,256]{2,1,0:T(8,128)(2,1)S(1)}, u32[]{:S(2)}, u32[]{:S(2)}) async-start(s16[16,80,256]{2,1,0:T(8,128)(2,1)} %bitcast.18), calls=%async_computation.2 | async-start | bytes 1310720 | tf_op jit(solution)/shard_map/all_to_all | solution.py:498
  84.5 2.6 %sum_features.1 = (s16[144,128]{1,0:T(8,128)(2,1)}, s16[128,128]{1,0:T(8,128)(2,1)}) custom-call(s16[2304,256]{1,0:T(8,128)(2,1)} %bitcast.14), custom_call_target="tpu_custom_call" | custom-call | flops 1048576 | bytes 2097152 | tf_op jit(solution)/shard_map/sum_features/pallas_call | solution.py:343
  87.1 2.8 %collective-permute-start.3 = (s16[144,128]{1,0:T(8,128)(2,1)}, s16[144,128]{1,0:T(8,128)(2,1)S(1)}, u32[]{:S(2)}, u32[]{:S(2)}) collective-permute-start(s16[144,128]{1,0:T(8,128)(2,1)} %get-tuple-element.18), channel_id=1, source_target_pairs={{0,16},{2,18},{4,20},{6,22},{8,24},{10,26},{12,28},{14,30},{16,0},... | collective-permute-start | bytes 110600 | tf_op jit(solution)/shard_map/ppermute | solution.py:360
  90.0 0.1 collective-permute-start.7
  90.1 0.8 constant_dynamic-update-slice_fusion.4
  90.8 0.8 constant_dynamic-update-slice_fusion.9
  91.6 11.7 %collective-permute-done.7 = s16[128,128]{1,0:T(8,128)(2,1)S(1)} collective-permute-done((s16[128,128]{1,0:T(8,128)(2,1)}, s16[128,128]{1,0:T(8,128)(2,1)S(1)}, u32[]{:S(2)}, u32[]{:S(2)}) %collective-permute-start.7) | collective-permute-done | bytes 32800 | tf_op jit(solution)/shard_map/ppermute | solution.py:360
  103.3 0.8 pad_add_fusion.5
  104.0 0.0 collective-permute-start.8
  104.0 0.8 pad_add_fusion.4
  104.8 2.0 %collective-permute-start.4 = (s16[288,128]{1,0:T(8,128)(2,1)S(1)}, s16[288,128]{1,0:T(8,128)(2,1)S(1)}, u32[]{:S(2)}, u32[]{:S(2)}) collective-permute-start(s16[288,128]{1,0:T(8,128)(2,1)S(1)} %pad_add_fusion.4), channel_id=1, source_target_pairs={{0,8},{2,10},{4,12},{6,14},{8,0},{10,2},{12,4},{14,6},{16,24},{18,... | collective-permute-start | bytes 221192 | tf_op jit(solution)/shard_map/ppermute | solution.py:360
  106.9 1.4 %collective-permute-done.8 = s16[256,128]{1,0:T(8,128)(2,1)S(1)} collective-permute-done((s16[256,128]{1,0:T(8,128)(2,1)S(1)}, s16[256,128]{1,0:T(8,128)(2,1)S(1)}, u32[]{:S(2)}, u32[]{:S(2)}) %collective-permute-start.8) | collective-permute-done | bytes 65568 | tf_op jit(solution)/shard_map/ppermute | solution.py:360
  108.3 0.8 pad_add_fusion.3
  109.1 1.5 %collective-permute-start.9 = (s16[512,128]{1,0:T(8,128)(2,1)S(1)}, s16[512,128]{1,0:T(8,128)(2,1)S(1)}, u32[]{:S(2)}, u32[]{:S(2)}) collective-permute-start(s16[512,128]{1,0:T(8,128)(2,1)S(1)} %pad_add_fusion.3), channel_id=1, source_target_pairs={{0,2},{2,0},{4,6},{6,4},{8,10},{10,8},{12,14},{14,12},{16,18},{18,... | collective-permute-start | bytes 393224 | tf_op jit(solution)/shard_map/ppermute | solution.py:360
  110.6 0.0 collective-permute-done.4
  110.6 0.8 pad_add_fusion.2
  111.4 1.5 %collective-permute-start.5 = (s16[576,128]{1,0:T(8,128)(2,1)S(1)}, s16[576,128]{1,0:T(8,128)(2,1)S(1)}, u32[]{:S(2)}, u32[]{:S(2)}) collective-permute-start(s16[576,128]{1,0:T(8,128)(2,1)S(1)} %pad_add_fusion.2), channel_id=1, source_target_pairs={{0,4},{2,6},{4,0},{6,2},{8,12},{10,14},{12,8},{14,10},{16,20},{18,... | collective-permute-start | bytes 442376 | tf_op jit(solution)/shard_map/ppermute | solution.py:360
  112.9 1.2 collective-permute-done.9
  114.1 0.8 pad_add_fusion.1
  114.9 1.5 %collective-permute-start.10 = (s16[1024,128]{1,0:T(8,128)(2,1)S(1)}, s16[1024,128]{1,0:T(8,128)(2,1)S(1)}, u32[]{:S(2)}, u32[]{:S(2)}) collective-permute-start(s16[1024,128]{1,0:T(8,128)(2,1)S(1)} %pad_add_fusion.1), channel_id=1, source_target_pairs={{0,4},{2,6},{4,0},{6,2},{8,12},{10,14},{12,8},{14,10},{16,20},{18,... | collective-permute-start | bytes 786440 | tf_op jit(solution)/shard_map/ppermute | solution.py:360
  116.4 0.0 all-to-all-done.2
  116.4 1.7 %collective-permute-done.5 = s16[576,128]{1,0:T(8,128)(2,1)S(1)} collective-permute-done((s16[576,128]{1,0:T(8,128)(2,1)S(1)}, s16[576,128]{1,0:T(8,128)(2,1)S(1)}, u32[]{:S(2)}, u32[]{:S(2)}) %collective-permute-start.5) | collective-permute-done | bytes 147488 | tf_op jit(solution)/shard_map/ppermute | solution.py:360
  118.2 0.8 pad_add_fusion
  119.0 0.7 collective-permute-start.6
  119.7 1.8 %collective-permute-done.10 = s16[1024,128]{1,0:T(8,128)(2,1)S(1)} collective-permute-done((s16[1024,128]{1,0:T(8,128)(2,1)S(1)}, s16[1024,128]{1,0:T(8,128)(2,1)S(1)}, u32[]{:S(2)}, u32[]{:S(2)}) %collective-permute-start.10) | collective-permute-done | bytes 262176 | tf_op jit(solution)/shard_map/ppermute | solution.py:360
  121.5 5.2 %collective-permute-done.6 = s16[1152,128]{1,0:T(8,128)(2,1)S(1)} collective-permute-done((s16[1152,128]{1,0:T(8,128)(2,1)S(1)}, s16[1152,128]{1,0:T(8,128)(2,1)S(1)}, u32[]{:S(2)}, u32[]{:S(2)}) %collective-permute-start.6) | collective-permute-done | bytes 294944 | tf_op jit(solution)/shard_map/ppermute | solution.py:360
  126.7 0.0 copy-start.1
  126.8 0.8 copy-done.1
  127.6 3.1 %decode_features.1 = f32[2048,256]{1,0:T(8,128)} custom-call(s32[1]{0:T(128)} %bitcast.11.w_ref, s16[2304,128]{1,0:T(8,128)(2,1)} %copy-done.1, s16[2048,128]{1,0:T(8,128)(2,1)} %copy-done.4), custom_call_target="tpu_custom_call" | custom-call | flops 1048576 | bytes 3145728 | tf_op jit(solution)/shard_map/decode_features/pallas_call | solution.py:385
  130.7 0.0 collective-permute-done.1.refs_3_
  130.7 0.5 copy-done.7
  131.3 0.3 copy-done.6
  131.6 7.2 %owner_sums.1 = (f32[2048,256]{1,0:T(8,128)}, f32[1024,256]{1,0:T(8,128)}, f32[32,256]{1,0:T(8,128)}) custom-call(s32[1]{0:T(128)} %bitcast.n_ref, s32[16,128]{1,0:T(8,128)} %bitcast.23, s32[16,128]{1,0:T(8,128)} %copy-done.7, s16[1280,256]{1,0:T(8,128)(2,1)} %bitcast.17, s16[1280,256]{1,0:T(8,128)(2,1)} %copy-done.6, ...), custom_call_target="tpu_custom_call" | custom-call | flops 6442450944 | bytes 8388608 | tf_op jit(solution)/shard_map/owner_sums/pallas_call | solution.py:467
  (24 shorter events, 0.2 us)
Async XLA Ops:
  22.4 23.5 %all-to-all-start.1 = ((bf16[16,80,256]{2,1,0:T(8,128)(2,1)}), bf16[16,80,256]{2,1,0:T(8,128)(2,1)S(1)}, u32[]{:S(2)}, u32[]{:S(2)}) async-start(bf16[16,80,256]{2,1,0:T(8,128)(2,1)} %bitcast.20), calls=%async_computation.1 | async-start | bytes 1310720 | tf_op jit(solution)/shard_map/all_to_all | solution.py:498
  45.9 13.1 %copy-start.3 = (bf16[16,80,256]{2,1,0:T(8,128)(2,1)}, bf16[16,80,256]{2,1,0:T(8,128)(2,1)S(1)}, u32[]{:S(2)}) copy-start(bf16[16,80,256]{2,1,0:T(8,128)(2,1)S(1)} %all-to-all-done.1) | copy-start | bytes 1966084
  45.9 32.3 %all-to-all-start.3 = ((s16[16,144,256]{2,1,0:T(8,128)(2,1)}), s16[16,144,256]{2,1,0:T(8,128)(2,1)S(1)}, u32[]{:S(2)}, u32[]{:S(2)}) async-start(s16[16,144,256]{2,1,0:T(8,128)(2,1)} %bitcast.15), calls=%async_computation.3 | async-start | bytes 2359296 | tf_op jit(solution)/shard_map/all_to_all | solution.py:498
  52.8 77.9 %collective-permute-start.2 = (f32[2048,256]{1,0:T(8,128)}, f32[2048,256]{1,0:T(8,128)}, u32[]{:S(2)}, u32[]{:S(2)}) collective-permute-start(f32[2048,256]{1,0:T(8,128)} %get-tuple-element.13), channel_id=1, source_target_pairs={{0,1},{1,0},{2,3},{3,2},{4,5},{5,4},{6,7},{7,6},{8,9},{9,8},{10,11... | collective-permute-start | bytes 6291464 | tf_op jit(solution)/shard_map/ppermute | solution.py:501
  52.9 6.1 %copy-start.5 = (s32[16,1,128]{2,1,0:T(1,128)S(1)}, s32[16,1,128]{2,1,0:T(1,128)}, u32[]{:S(2)}) copy-start(s32[16,1,128]{2,1,0:T(1,128)} %all_to_all.44) | copy-start | bytes 24580
  59.0 71.7 %collective-permute-start = (s32[16,128]{1,0:T(8,128)S(1)}, s32[16,128]{1,0:T(8,128)S(1)}, u32[]{:S(2)}, u32[]{:S(2)}) collective-permute-start(s32[16,128]{1,0:T(8,128)S(1)} %bitcast.24), channel_id=1, source_target_pairs={{0,1},{1,0},{2,3},{3,2},{4,5},{5,4},{6,7},{7,6},{8,9},{9,8},{10,11... | collective-permute-start | bytes 24584 | tf_op jit(solution)/shard_map/ppermute | solution.py:501
  78.2 6.3 %copy-start = (s16[16,144,256]{2,1,0:T(8,128)(2,1)}, s16[16,144,256]{2,1,0:T(8,128)(2,1)S(1)}, u32[]{:S(2)}) copy-start(s16[16,144,256]{2,1,0:T(8,128)(2,1)S(1)} %all-to-all-done.3) | copy-start | bytes 3538948
  78.2 38.2 %all-to-all-start.2 = ((s16[16,80,256]{2,1,0:T(8,128)(2,1)}), s16[16,80,256]{2,1,0:T(8,128)(2,1)S(1)}, u32[]{:S(2)}, u32[]{:S(2)}) async-start(s16[16,80,256]{2,1,0:T(8,128)(2,1)} %bitcast.18), calls=%async_computation.2 | async-start | bytes 1310720 | tf_op jit(solution)/shard_map/all_to_all | solution.py:498
  87.1 16.9 %collective-permute-start.3 = (s16[144,128]{1,0:T(8,128)(2,1)}, s16[144,128]{1,0:T(8,128)(2,1)S(1)}, u32[]{:S(2)}, u32[]{:S(2)}) collective-permute-start(s16[144,128]{1,0:T(8,128)(2,1)} %get-tuple-element.18), channel_id=1, source_target_pairs={{0,16},{2,18},{4,20},{6,22},{8,24},{10,26},{12,28},{14,30},{16,0},... | collective-permute-start | bytes 110600 | tf_op jit(solution)/shard_map/ppermute | solution.py:360
  90.0 13.3 %collective-permute-start.7 = (s16[128,128]{1,0:T(8,128)(2,1)}, s16[128,128]{1,0:T(8,128)(2,1)S(1)}, u32[]{:S(2)}, u32[]{:S(2)}) collective-permute-start(s16[128,128]{1,0:T(8,128)(2,1)} %get-tuple-element.19), channel_id=1, source_target_pairs={{0,16},{2,18},{4,20},{6,22},{8,24},{10,26},{12,28},{14,30},{16,0},... | collective-permute-start | bytes 98312 | tf_op jit(solution)/shard_map/ppermute | solution.py:360
  104.0 4.3 %collective-permute-start.8 = (s16[256,128]{1,0:T(8,128)(2,1)S(1)}, s16[256,128]{1,0:T(8,128)(2,1)S(1)}, u32[]{:S(2)}, u32[]{:S(2)}) collective-permute-start(s16[256,128]{1,0:T(8,128)(2,1)S(1)} %pad_add_fusion.5), channel_id=1, source_target_pairs={{0,8},{2,10},{4,12},{6,14},{8,0},{10,2},{12,4},{14,6},{16,24},{18,... | collective-permute-start | bytes 196616 | tf_op jit(solution)/shard_map/ppermute | solution.py:360
  104.8 5.8 %collective-permute-start.4 = (s16[288,128]{1,0:T(8,128)(2,1)S(1)}, s16[288,128]{1,0:T(8,128)(2,1)S(1)}, u32[]{:S(2)}, u32[]{:S(2)}) collective-permute-start(s16[288,128]{1,0:T(8,128)(2,1)S(1)} %pad_add_fusion.4), channel_id=1, source_target_pairs={{0,8},{2,10},{4,12},{6,14},{8,0},{10,2},{12,4},{14,6},{16,24},{18,... | collective-permute-start | bytes 221192 | tf_op jit(solution)/shard_map/ppermute | solution.py:360
  109.1 5.0 %collective-permute-start.9 = (s16[512,128]{1,0:T(8,128)(2,1)S(1)}, s16[512,128]{1,0:T(8,128)(2,1)S(1)}, u32[]{:S(2)}, u32[]{:S(2)}) collective-permute-start(s16[512,128]{1,0:T(8,128)(2,1)S(1)} %pad_add_fusion.3), channel_id=1, source_target_pairs={{0,2},{2,0},{4,6},{6,4},{8,10},{10,8},{12,14},{14,12},{16,18},{18,... | collective-permute-start | bytes 393224 | tf_op jit(solution)/shard_map/ppermute | solution.py:360
  111.4 6.8 %collective-permute-start.5 = (s16[576,128]{1,0:T(8,128)(2,1)S(1)}, s16[576,128]{1,0:T(8,128)(2,1)S(1)}, u32[]{:S(2)}, u32[]{:S(2)}) collective-permute-start(s16[576,128]{1,0:T(8,128)(2,1)S(1)} %pad_add_fusion.2), channel_id=1, source_target_pairs={{0,4},{2,6},{4,0},{6,2},{8,12},{10,14},{12,8},{14,10},{16,20},{18,... | collective-permute-start | bytes 442376 | tf_op jit(solution)/shard_map/ppermute | solution.py:360
  114.9 6.5 %collective-permute-start.10 = (s16[1024,128]{1,0:T(8,128)(2,1)S(1)}, s16[1024,128]{1,0:T(8,128)(2,1)S(1)}, u32[]{:S(2)}, u32[]{:S(2)}) collective-permute-start(s16[1024,128]{1,0:T(8,128)(2,1)S(1)} %pad_add_fusion.1), channel_id=1, source_target_pairs={{0,4},{2,6},{4,0},{6,2},{8,12},{10,14},{12,8},{14,10},{16,20},{18,... | collective-permute-start | bytes 786440 | tf_op jit(solution)/shard_map/ppermute | solution.py:360
  116.4 14.3 %copy-start.2 = (s16[16,80,256]{2,1,0:T(8,128)(2,1)}, s16[16,80,256]{2,1,0:T(8,128)(2,1)S(1)}, u32[]{:S(2)}) copy-start(s16[16,80,256]{2,1,0:T(8,128)(2,1)S(1)} %all-to-all-done.2) | copy-start | bytes 1966084
  116.4 14.3 %collective-permute-start.1 = (s16[1280,256]{1,0:T(8,128)(2,1)S(1)}, s16[1280,256]{1,0:T(8,128)(2,1)S(1)}, u32[]{:S(2)}, u32[]{:S(2)}) collective-permute-start(s16[1280,256]{1,0:T(8,128)(2,1)S(1)} %bitcast.16), channel_id=1, source_target_pairs={{0,1},{1,0},{2,3},{3,2},{4,5},{5,4},{6,7},{7,6},{8,9},{9,8},{10,11... | collective-permute-start | bytes 1966088 | tf_op jit(solution)/shard_map/ppermute | solution.py:501
  119.0 7.7 %collective-permute-start.6 = (s16[1152,128]{1,0:T(8,128)(2,1)S(1)}, s16[1152,128]{1,0:T(8,128)(2,1)S(1)}, u32[]{:S(2)}, u32[]{:S(2)}) collective-permute-start(s16[1152,128]{1,0:T(8,128)(2,1)S(1)} %pad_add_fusion), channel_id=1, source_target_pairs={{0,2},{2,0},{4,6},{6,4},{8,10},{10,8},{12,14},{14,12},{16,18},{18,... | collective-permute-start | bytes 884744 | tf_op jit(solution)/shard_map/ppermute | solution.py:360
  121.5 5.3 %copy-start.4 = (s16[2048,128]{1,0:T(8,128)(2,1)}, s16[2048,128]{1,0:T(8,128)(2,1)S(1)}, u32[]{:S(2)}) copy-start(s16[2048,128]{1,0:T(8,128)(2,1)S(1)} %constant_dynamic-update-slice_fusion.5.b_ref) | copy-start | bytes 1572868
  126.7 0.8 copy-start.1
  130.7 0.6 copy-start.7
  130.7 0.9 copy-start.6

commit v2 on v1

--- a/solution.py
+++ b/solution.py
@@ -17,6 +17,7 @@
 CAPW = 4
 SLOT = 80
 TAIL = 16
+PLANE = 4
 HALF = 14
 F32, BF16, I32, I16 = jnp.float32, jnp.bfloat16, jnp.int32, jnp.int16
 NN = (((1,), (0,)), ((), ()))
@@ -32,12 +33,16 @@
     return lax.broadcasted_iota(I32, shape, dim)
 
 
-def params(**kw):
-    return pltpu.CompilerParams(vmem_limit_bytes=56 << 20, **kw)
+def params(mib, **kw):
+    return pltpu.CompilerParams(vmem_limit_bytes=mib << 20, **kw)
 
 
 def cost(flops, nbytes):
     return pl.CostEstimate(flops=flops, bytes_accessed=nbytes, transcendentals=0)
+
+
+def busy(us):
+    return cost(us * 1_150_000_000, 0)
 
 
 VM = pl.BlockSpec(memory_space=pltpu.VMEM)
@@ -55,6 +60,27 @@
 
 def column_of(row):
     return jnp.broadcast_to(row, (128, 128)).T[:, :1]
+
+
+def request_kernel(u_ref, v_ref, wt_ref, out_ref, flip):
+    out_ref[...] = jnp.zeros_like(out_ref)
+    out_ref[:, :CAPU] = u_ref[...]
+    out_ref[:, CAPU : CAPU + CAPI] = v_ref[...]
+    flip[...] = jnp.zeros_like(flip)
+    flip[:CAPW, : wt_ref.shape[1]] = wt_ref[...]
+    out_ref[:, CAPU + CAPI : CAPU + CAPI + CAPW] = flip[...].T[: out_ref.shape[0], :CAPW]
+
+
+def requests(u, v, w):
+    return pl.pallas_call(
+        request_kernel,
+        in_specs=[VM] * 3,
+        out_specs=VM,
+        out_shape=jax.ShapeDtypeStruct((u.shape[0], 128), I32),
+        scratch_shapes=[pltpu.VMEM((128, 128), I32)],
+        compiler_params=params(58),
+        name="requests",
+    )(u, v, w.T)
 
 
 def gather_kernel(owners, got_ref, ut_ref, it_ref, wt_ref, out_ref):
@@ -88,8 +114,8 @@
         in_specs=[VM] * 4,
         out_specs=VM,
         out_shape=jax.ShapeDtypeStruct((owners * SLOT, RANK), BF16),
-        compiler_params=params(),
-        cost_estimate=cost(2 << 30, 4 << 20),
+        compiler_params=params(58),
+        cost_estimate=busy(5),
         name="gather_rows",
     )(got, ut, it, wt)
 
@@ -133,8 +159,8 @@
         in_specs=[VM],
         out_specs=VM,
         out_shape=jax.ShapeDtypeStruct((BU, BI), I32),
-        compiler_params=params(),
-        cost_estimate=cost(4 << 30, 1 << 20),
+        compiler_params=params(12),
+        cost_estimate=busy(6),
         name="positives",
     )(pos.reshape(-1, 128))
 
@@ -165,6 +191,7 @@
     v, hit_v, into_v = listed(vc_ref, CAPI, CAPI, CAPU, BI)
     w, hit_w, into_w = listed(wc_ref, CAPW, TAIL, CAPU + CAPI, BWP)
     vb = v.astype(BF16)
+    vt = v.T.astype(BF16)
     ut = u.T
     wt = jnp.concatenate([w, jnp.zeros((128 - BWP, RANK), F32)], axis=0).T
     gw[...] = jnp.zeros_like(gw)
@@ -172,7 +199,7 @@
     for k in range(BW):
         wk = w[k : k + 1, :]
         uw = (u * wk).astype(BF16)
-        m = mm(uw, vb, NT)
+        m = mm(uw, vt)
         pos = ((bits[...] >> k) & 1).astype(F32)
         g = (1.0 / (1.0 + jnp.exp(-m)) - pos).astype(BF16)
         q = mm(g, vb)
@@ -228,13 +255,13 @@
         out_specs=VM,
         out_shape=jax.ShapeDtypeStruct((owners * SLOT, RANK), I16),
         scratch_shapes=[pltpu.VMEM((BU, RANK), F32), pltpu.VMEM((RANK, BI), F32), pltpu.VMEM((BWP, RANK), F32)],
-        compiler_params=params(),
-        cost_estimate=cost(4 << 30, 2 << 20),
+        compiler_params=params(20),
+        cost_estimate=busy(30),
         name="block_slots",
     )(back, bits, uc, vc, wc)
 
 
-def dense_kernel(shares, per, chunk, n_ref, x_ref, u_ref, f_ref, others_ref, mine_ref, gf_ref, acc):
+def dense_kernel(shares, per, chunk, n_ref, w_ref, x_ref, u_ref, f_ref, others_ref, mine_ref, own_ref, g1, g2, g3, acc, ft):
     t = pl.program_id(0)
     u = u_ref[...]
     nf = f_ref.shape[0]
@@ -242,11 +269,12 @@
     @pl.when(t == 0)
     def _():
         acc[...] = jnp.zeros_like(acc)
+        ft[...] = f_ref[...].astype(F32).T.astype(BF16)
 
     total = None
     for c in range(0, nf, chunk):
         f = f_ref[c : c + chunk, :]
-        r = (mm(u, f, NT) - x_ref[:, c : c + chunk].astype(F32)).astype(BF16)
+        r = (mm(u, ft[:, c : c + chunk]) - x_ref[:, c : c + chunk].astype(F32)).astype(BF16)
         part = mm(r, f)
         total = part if total is None else total + part
         acc[c : c + chunk, :] += mm(r, u, TN)
@@ -261,136 +289,137 @@
 
     @pl.when(t == pl.num_programs(0) - 1)
     def _():
-        pack_features(0.0625 * acc[...], gf_ref)
-
-
-def pack_features(g, out_ref):
-    nf = g.shape[0]
-    c = nf // 16
-    eye = iota((c, 128), 0) == iota((c, 128), 1)
-    for o in range(16):
-        part = g[c * o : c * (o + 1)]
-        e = row_exponent(part)
-        q = jnp.round(part * pow2(14.0 - e))
-        row = jnp.sum(jnp.where(eye, e, 0.0), axis=0, keepdims=True)
-        row = jnp.concatenate([row, row], axis=1)
-        b = (c + TAIL) * o
-        out_ref[b : b + c, :] = q.astype(I32).astype(I16)
-        tail = jnp.where(iota((TAIL, RANK), 0) == 8, row, 0.0)
-        out_ref[b + c : b + c + TAIL, :] = tail.astype(I32).astype(I16)
-
-
-def dense(n, x, u, f, shares):
+        share_out(acc, 0.0625, nf // PLANE, lax.rem(w_ref[0], PLANE), own_ref, (g1, g2, g3))
+
+
+def share_out(ref, factor, r, me, own_ref, outs):
+    def part(m):
+        return factor * ref[pl.ds(pl.multiple_of((me ^ m) * r, r), r), :]
+
+    own_ref[...] = part(0)
+    for m in range(1, 4):
+        pack(part(m), outs[m - 1], 0)
+
+
+def pack(g, out_ref, base):
+    r = g.shape[0]
+    e = row_exponent(g)
+    q = jnp.round(g * pow2(14.0 - e))
+    out_ref[base : base + r, :] = q.astype(I32).astype(I16)
+    tail = jnp.zeros((TAIL, RANK), F32)
+    sub = iota((TAIL, RANK), 0)
+    step = min(r, 128)
+    eye = iota((step, 128), 0) == iota((step, 128), 1)
+    for i in range(r // step):
+        row = jnp.sum(jnp.where(eye, e[step * i : step * (i + 1)], 0.0), axis=0, keepdims=True)
+        tail = jnp.where(sub == 8 + i, jnp.concatenate([row, row], axis=1), tail)
+    out_ref[base + r : base + r + TAIL, :] = tail.astype(I32).astype(I16)
+
+
+def unpack(ref, base, r):
+    q = ref[base : base + r, :].astype(I32).astype(F32)
+    tail = ref[base + r : base + r + TAIL, :].astype(I32).astype(F32)
+    step = min(r, 128)
+    e = [column_of(tail[8 + i : 9 + i, :128])[:step] for i in range(r // step)]
+    return q * pow2(jnp.concatenate(e, axis=0) - 14.0)
+
+
+def dense(n, w, x, u, f, shares):
     nu, nf = x.shape
     own = nu // shares
     tile = 512
     per = own // tile
     tiles = nu // tile
 
-    def rows(t, n_ref):
+    def rows(t, n_ref, w_ref):
         return (lax.rem(n_ref[0] + 1 + t // per, shares) * per + lax.rem(t, per), 0)
 
     return pl.pallas_call(
         functools.partial(dense_kernel, shares, per, nf),
         grid_spec=pltpu.PrefetchScalarGridSpec(
-            num_scalar_prefetch=1,
+            num_scalar_prefetch=2,
             grid=(tiles,),
             in_specs=[
                 pl.BlockSpec((tile, nf), rows),
                 pl.BlockSpec((tile, RANK), rows),
-                pl.BlockSpec((nf, RANK), lambda t, n_ref: (0, 0)),
+                pl.BlockSpec((nf, RANK), lambda t, n_ref, w_ref: (0, 0)),
             ],
             out_specs=[
-                pl.BlockSpec((tile, RANK), lambda t, n_ref: (jnp.minimum(t, (shares - 1) * per - 1), 0)),
-                pl.BlockSpec((tile, RANK), lambda t, n_ref: (jnp.maximum(t - (shares - 1) * per, 0), 0)),
-                pl.BlockSpec((nf + 16 * TAIL, RANK), lambda t, n_ref: (0, 0)),
-            ],
-            scratch_shapes=[pltpu.VMEM((nf, RANK), F32)],
+                pl.BlockSpec((tile, RANK), lambda t, n_ref, w_ref: (jnp.minimum(t, (shares - 1) * per - 1), 0)),
+                pl.BlockSpec((tile, RANK), lambda t, n_ref, w_ref: (jnp.maximum(t - (shares - 1) * per, 0), 0)),
+                pl.BlockSpec((nf // PLANE, RANK), lambda t, n_ref, w_ref: (0, 0)),
+            ]
+            + [pl.BlockSpec((nf // PLANE + TAIL, RANK), lambda t, n_ref, w_ref: (0, 0))] * 3,
+            scratch_shapes=[pltpu.VMEM((nf, RANK), F32), pltpu.VMEM((RANK, nf), BF16)],
         ),
         out_shape=[
             jax.ShapeDtypeStruct(((shares - 1) * own, RANK), F32),
             jax.ShapeDtypeStruct((own, RANK), F32),
-            jax.ShapeDtypeStruct((nf + 16 * TAIL, RANK), I16),
-        ],
-        compiler_params=params(dimension_semantics=("arbitrary",)),
+            jax.ShapeDtypeStruct((nf // PLANE, RANK), F32),
+        ]
+        + [jax.ShapeDtypeStruct((nf // PLANE + TAIL, RANK), I16)] * 3,
+        compiler_params=params(58, dimension_semantics=("arbitrary",)),
         cost_estimate=cost(3 * 2 * nu * nf * RANK, 2 * nu * nf + 8 * nu * RANK),
         name="dense",
-    )(n, x, u, f)
-
-
-def unpacked(block, c):
-    q = block[:c].astype(I32).astype(F32)
-    e = block[c : c + TAIL].astype(I32).astype(F32)[8:9, :128]
-    return q * pow2(column_of(e)[:c] - 14.0)
-
-
-def sum_kernel(c, in_ref, a_ref, b_ref):
-    total = None
-    for o in range(16):
-        part = unpacked(in_ref[(c + TAIL) * o : (c + TAIL) * (o + 1), :], c)
-        total = part if total is None else total + part
-    e = row_exponent(total)
-    q = jnp.round(total * pow2(14.0 - e)).astype(I32)
-    eye = iota((c, 128), 0) == iota((c, 128), 1)
-    row = jnp.sum(jnp.where(eye, e, 0.0), axis=0, keepdims=True)
-    tail = jnp.where(iota((TAIL, 128), 0) == 8, row, 0.0)
-    a_ref[:c, :] = q[:, :128].astype(I16)
-    a_ref[c:, :] = tail.astype(I32).astype(I16)
-    b_ref[...] = q[:, 128:].astype(I16)
-
-
-def sum_features(parts, c):
-    return pl.pallas_call(
-        functools.partial(sum_kernel, c),
-        in_specs=[VM],
-        out_specs=[VM, VM],
-        out_shape=[jax.ShapeDtypeStruct((c + TAIL, 128), I16), jax.ShapeDtypeStruct((c, 128), I16)],
-        compiler_params=params(),
-        cost_estimate=cost(1 << 20, 2 << 20),
-        name="sum_features",
-    )(parts)
-
-
-ORDER_A = (8, 4, 2, 1)
-ORDER_B = (8, 4, 1, 2)
-
-
-def spread(x, order):
-    for bit in order:
-        x = jnp.concatenate([x, lax.ppermute(x, "wide", [(i, i ^ bit) for i in range(16)])], axis=0)
-    return x
-
-
-def flips(order):
-    out = []
-    for j in range(16):
-        out.append(sum(bit for i, bit in enumerate(order) if (j >> i) & 1))
-    return out
-
-
-def decode_kernel(c, w_ref, a_ref, b_ref, out_ref):
-    me = w_ref[0]
-    at_b = flips(ORDER_B)
-    for j, flip in enumerate(flips(ORDER_A)):
-        i = at_b.index(flip)
-        base = (c + TAIL) * j
-        e = a_ref[base + c : base + c + TAIL, :].astype(I32).astype(F32)[8:9, :]
-        scale = pow2(column_of(e)[:c] - 14.0)
-        at = pl.multiple_of((me ^ flip) * c, c)
-        out_ref[pl.ds(at, c), :128] = a_ref[base : base + c, :].astype(I32).astype(F32) * scale
-        out_ref[pl.ds(at, c), 128:] = b_ref[c * i : c * (i + 1), :].astype(I32).astype(F32) * scale
-
-
-def decode_features(w, a, b, c):
+    )(n, w, x, u, f)
+
+
+def sum_kernel(r, w_ref, own_ref, in1, in2, in3, out_ref, g1, g2, g3, total):
+    total[...] = (own_ref[...] + unpack(in1, 0, r)) + (unpack(in2, 0, r) + unpack(in3, 0, r))
+    share_out(total, 1.0, r // 4, w_ref[0] // PLANE, out_ref, (g1, g2, g3))
+
+
+def sum_plane(w, own, parts):
+    r = own.shape[0]
+    return pl.pallas_call(
+        functools.partial(sum_kernel, r),
+        in_specs=[SM] + [VM] * 4,
+        out_specs=[VM] * 4,
+        out_shape=[jax.ShapeDtypeStruct((r // 4, RANK), F32)]
+        + [jax.ShapeDtypeStruct((r // 4 + TAIL, RANK), I16)] * 3,
+        scratch_shapes=[pltpu.VMEM((r, RANK), F32)],
+        compiler_params=params(12),
+        cost_estimate=busy(25),
+        name="sum_plane",
+    )(w, own, *parts)
+
+
+def last_kernel(c, own_ref, in1, in2, in3, out_ref):
+    pack((own_ref[...] + unpack(in1, 0, c)) + (unpack(in2, 0, c) + unpack(in3, 0, c)), out_ref, 0)
+
+
+def sum_line(own, parts):
+    c = own.shape[0]
+    return pl.pallas_call(
+        functools.partial(last_kernel, c),
+        in_specs=[VM] * 4,
+        out_specs=VM,
+        out_shape=jax.ShapeDtypeStruct((c + TAIL, RANK), I16),
+        compiler_params=params(12),
+        cost_estimate=busy(25),
+        name="sum_line",
+    )(own, *parts)
+
+
+def decode_kernel(c, w_ref, *refs):
+    out_ref = refs[-1]
+    place, height = w_ref[0] % PLANE, w_ref[0] // PLANE
+    for m in range(PLANE):
+        for z in range(4):
+            at = pl.multiple_of(((place ^ m) * 4 + (height ^ z)) * c, c)
+            out_ref[pl.ds(at, c), :] = unpack(refs[m], (c + TAIL) * z, c)
+
+
+def decode_features(w, parts, c):
     return pl.pallas_call(
         functools.partial(decode_kernel, c),
-        in_specs=[SM, VM, VM],
+        in_specs=[SM] + [VM] * PLANE,
         out_specs=VM,
         out_shape=jax.ShapeDtypeStruct((16 * c, RANK), F32),
-        compiler_params=params(),
+        compiler_params=params(12),
         cost_estimate=cost(1 << 20, 3 << 20),
         name="decode_features",
-    )(w, a, b)
+    )(w, *parts)
 
 
 def lanes(x, width, off):
@@ -469,8 +498,8 @@
         in_specs=[SM] + [VM] * (3 * shares),
         out_specs=[VM] * 3,
         out_shape=[jax.ShapeDtypeStruct((r, RANK), F32) for r in (own_u, own_i, own_w)],
-        compiler_params=params(),
-        cost_estimate=cost(6 << 30, 8 << 20),
+        compiler_params=params(28),
+        cost_estimate=busy(30),
         name="owner_sums",
     )(n, *gots, *rets, *parts)
 
@@ -494,28 +523,41 @@
     n = lax.axis_index("narrow").astype(I32).reshape(1)
     w = lax.axis_index("wide").astype(I32).reshape(1)
 
+    def flip(x, bits):
+        return lax.ppermute(x, "wide", [(i, i ^ bits) for i in range(owners)])
+
     def across(x):
         return lax.all_to_all(x, "wide", split_axis=0, concat_axis=0, tiled=True)
 
     def shift(x, r):
         return lax.ppermute(x, "narrow", [(i, (i + r) % shares) for i in range(shares)])
 
-    spare = jnp.zeros((owners, 128 - CAPU - CAPI - CAPW), I32)
-    got = across(jnp.concatenate([user_req[0], item_req[0], week_req[0], spare], axis=1))
-    back = across(gather_rows(got, user_table, item_table, week_table))
+    tie = lax.optimization_barrier
+    got = across(requests(user_req[0], item_req[0], week_req[0]))
     bits = positives(pos_cells[0])
-    others, mine, packed = dense(n, profile, user_table, feature_table, shares)
+    got, bits = tie((got, bits))
+    n, rows = tie((n, gather_rows(got, user_table, item_table, week_table)))
+    back = across(rows)
+    others, mine, own, *packed = dense(n, w, profile, user_table, feature_table, shares)
     own_u = mine.shape[0]
-    c = feature_table.shape[0] // 16
-    shard_a, shard_b = sum_features(across(packed), c)
-    grad_features = decode_features(w, spread(shard_a, ORDER_A), spread(shard_b, ORDER_B), c)
-    ret = across(block_slots(back, bits, user_counts, item_counts, week_counts))
+    back, own = tie((back, own))
+    slots = block_slots(back, bits, user_counts, item_counts, week_counts)
+    packed = [flip(x, m + 1) for m, x in enumerate(packed)]
+    own, slots = tie((own, slots))
+    own, *packed = sum_plane(w, own, packed)
+    ret = across(slots)
+    mark = sum_line(own, [flip(x, PLANE * (m + 1)) for m, x in enumerate(packed)])
+    known = jnp.concatenate([mark] + [flip(mark, PLANE * m) for m in range(1, 4)], axis=0)
+    ret, known = tie((ret, known))
+    knowns = [known] + [flip(known, m) for m in range(1, PLANE)]
     gots = [got] + [shift(got, r) for r in range(1, shares)]
     rets = [ret] + [shift(ret, r) for r in range(1, shares)]
     parts = [mine] + [shift(others[own_u * (r - 1) : own_u * r], r) for r in range(1, shares)]
     grad_users, grad_items, grad_weeks = owner_sums(
         n, gots, rets, parts, own_u, item_table.shape[0] // shares, week_table.shape[0] // shares
     )
+    w, grad_weeks = tie((w, grad_weeks))
+    grad_features = decode_features(w, knowns, feature_table.shape[0] // owners)
     return (grad_users, grad_items, grad_weeks, grad_features)
 
 

time: 140 us -> 117 us (0.84)
  blocking collectives: 15.3 us -> 0 us
  starting transfers between devices: 27.5 us -> 36 us
  other arithmetic: 5.44 us -> 0.02 us
  Pallas kernels: 51.9 us -> 46.6 us
  waiting for transfers between devices: 33.6 us -> 29.8 us
    all_to_all x1 -> x0, blocking collectives: 15.3 us -> none  [across(): return lax.all_to_all(x, 'wide', split_axis=0, concat_axis=0, tiled=True)]
    all_to_all x3, waiting for transfers between devices: 10.6 us -> 1.78 us  [across(): return lax.all_to_all(x, 'wide', split_axis=0, concat_axis=0, tiled=True)]
    ppermute x8 -> x12, starting transfers between devices: 10.2 us -> 16.4 us  [flip(): return lax.ppermute(x, 'wide', [(i, i ^ bits) for i in range(owners)])]
    concatenate x7 -> x1, other arithmetic: 5.44 us -> 0.02 us  [local(): jnp.concatenate([mark] + [flip(mark, PLANE * m) for m in range(1, 4)], ax...]
    ppermute x8 -> x12, waiting for transfers between devices: 23 us -> 28 us  [flip(): return lax.ppermute(x, 'wide', [(i, i ^ bits) for i in range(owners)])]
    all_to_all x3, starting transfers between devices: 16.7 us -> 19 us  [across(): return lax.all_to_all(x, 'wide', split_axis=0, concat_axis=0, tiled=True)]
    pallas_call x1, Pallas kernels: 7.19 us -> 5.19 us  [owner_sums(): pl.pallas_call(functools.partial(owner_kernel, shares), in_specs=[SM] + [...]
    pallas_call x1, Pallas kernels: 6.1 us -> 4.69 us  [positives(): pl.pallas_call(positives_kernel, in_specs=[VM], out_specs=VM, out_shape=j...]
  transfers between devices with their start and end apart: 14 -> 18, of which waited for: 7 -> 5; matrix products, arithmetic and copies ran while one was open for 5% -> 0% of each run, Pallas kernels for 29% -> 32%
where the time goes in v2:
time: 117 us; the launch traced here: 116 us
  Pallas kernels  46.6 us (40%)
  starting transfers between devices  36 us (31%)
  waiting for transfers between devices  29.8 us (25%)
  local copies, waits for them, and re-layouts  2.93 us (3%)
    ppermute x12, waiting for transfers between devices, flip(): return lax.ppermute(x, 'wide', [(i, i ^ bits) for i in range(owners)])  28 us
    pallas_call x1, Pallas kernels, dense(): pl.pallas_call(functools.partial(dense_kernel, shares, per, nf), grid_spe...  19.9 us
    all_to_all x3, starting transfers between devices, across(): return lax.all_to_all(x, 'wide', split_axis=0, concat_axis=0, tiled=True)  19 us
    ppermute x12, starting transfers between devices, flip(): return lax.ppermute(x, 'wide', [(i, i ^ bits) for i in range(owners)])  16.4 us
    pallas_call x1, Pallas kernels, block_slots(): pl.pallas_call(functools.partial(block_kernel, owners), in_specs=[VM, VM,...  7.55 us
    pallas_call x1, Pallas kernels, owner_sums(): pl.pallas_call(functools.partial(owner_kernel, shares), in_specs=[SM] + [...  5.19 us
    pallas_call x1, Pallas kernels, gather_rows(): pl.pallas_call(functools.partial(gather_kernel, owners), in_specs=[VM] *...  4.84 us
    pallas_call x1, Pallas kernels, positives(): pl.pallas_call(positives_kernel, in_specs=[VM], out_specs=VM, out_shape=j...  4.69 us
  transfers between devices with their start and end apart: 18, of which 5 were waited for; matrix products, arithmetic and copies ran while one was open for 0% of the time, Pallas kernels for 32%

profile of v2, /device:TPU:0, one launch (start us, length us, event | category | flops | bytes accessed | tf_op | source)
XLA Modules:
  0.0 116.1 jit_solution(15337985026197870996)
XLA Ops:
  0.6 1.5 %requests.1 = s32[16,128]{1,0:T(8,128)} custom-call(s32[16,32]{1,0:T(8,128)} %bitcast.25, s32[16,32]{1,0:T(8,128)} %bitcast.26, s32[4,16]{1,0:T(4,128)} %bitcast.27), custom_call_target="tpu_custom_call" | custom-call | tf_op jit(solution)/shard_map/requests/pallas_call | solution.py:75
  2.1 8.3 %all-to-all-start = ((s32[16,1,128]{2,1,0:T(1,128)}), s32[16,1,128]{2,1,0:T(1,128)S(1)}, u32[]{:S(2)}, u32[]{:S(2)}) async-start(s32[16,1,128]{2,1,0:T(1,128)} %bitcast.24), calls=%async_computation | async-start | bytes 16384 | tf_op jit(solution)/shard_map/all_to_all | solution.py:530
  10.4 0.0 copy-start.2
  10.4 0.7 copy-done.2
  11.1 4.7 %positives.1.bits_ref = s32[256,256]{1,0:T(8,128)S(1)} custom-call(s32[32,128]{1,0:T(8,128)S(1)} %bitcast.22), custom_call_target="tpu_custom_call" | custom-call | flops 6899999744 | tf_op jit(solution)/shard_map/positives/pallas_call | solution.py:157
  15.8 1.8 %all-to-all-done = s32[16,1,128]{2,1,0:T(1,128)S(1)} async-done(((s32[16,1,128]{2,1,0:T(1,128)}), s32[16,1,128]{2,1,0:T(1,128)S(1)}, u32[]{:S(2)}, u32[]{:S(2)}) %all-to-all-start) | async-done | bytes 8224 | tf_op jit(solution)/shard_map/all_to_all | solution.py:530
  17.6 0.6 copy-done
  18.2 4.8 %gather_rows.1 = bf16[1280,256]{1,0:T(8,128)(2,1)} custom-call(s32[16,128]{1,0:T(8,128)} %bitcast.19, bf16[4096,256]{1,0:T(8,128)(2,1)} %u_ref.1, bf16[2048,256]{1,0:T(8,128)(2,1)} %it_ref.1, bf16[64,256]{1,0:T(8,128)(2,1)} %wt_ref.1), custom_call_target="tpu_custom_call" | custom-call | flops 5750000128 | tf_op jit(solution)/shard_map/gather_rows/pallas_call | solution.py:112
  23.0 5.2 %all-to-all-start.1 = ((bf16[16,80,256]{2,1,0:T(8,128)(2,1)}), bf16[16,80,256]{2,1,0:T(8,128)(2,1)S(1)}, u32[]{:S(2)}, u32[]{:S(2)}) async-start(bf16[16,80,256]{2,1,0:T(8,128)(2,1)} %bitcast.23), calls=%async_computation.1 | async-start | bytes 1310720 | tf_op jit(solution)/shard_map/all_to_all | solution.py:530
  28.2 0.0 copy-start.3
  28.2 0.0 copy-start.4
  28.2 0.0 copy-start.5
  28.3 19.9 %dense.1 = (f32[2048,256]{1,0:T(8,128)}, f32[2048,256]{1,0:T(8,128)}, f32[512,256]{1,0:T(8,128)}, s16[528,256]{1,0:T(8,128)(2,1)}, s16[528,256]{1,0:T(8,128)(2,1)}, /*index=5*/s16[528,256]{1,0:T(8,128)(2,1)}) custom-call(s32[1]{0:T(128)} %bitcast.n_ref, s32[1]{0:T(128)} %bitcast.11.w_ref, bf16[4096,2048]{1,0:T(8,128)(2,1)} %x_ref.1, ...), custom_call_target="tpu_custom_call" | custom-call | flops 12884901888 | bytes 25165824 | tf_op jit(solution)/shard_map/dense/pallas_call | solution.py:337
  48.2 2.0 %collective-permute-start.1 = (s16[528,256]{1,0:T(8,128)(2,1)}, s16[528,256]{1,0:T(8,128)(2,1)S(1)}, u32[]{:S(2)}, u32[]{:S(2)}) collective-permute-start(s16[528,256]{1,0:T(8,128)(2,1)} %get-tuple-element.38), channel_id=1, source_target_pairs={{0,2},{2,0},{4,6},{6,4},{8,10},{10,8},{12,14},{14,12},{16,18},{18,... | collective-permute-start | bytes 811016 | tf_op jit(solution)/shard_map/ppermute | solution.py:527
  50.1 1.5 %collective-permute-start.2 = (s16[528,256]{1,0:T(8,128)(2,1)}, s16[528,256]{1,0:T(8,128)(2,1)S(1)}, u32[]{:S(2)}, u32[]{:S(2)}) collective-permute-start(s16[528,256]{1,0:T(8,128)(2,1)} %get-tuple-element.39), channel_id=1, source_target_pairs={{0,4},{2,6},{4,0},{6,2},{8,12},{10,14},{12,8},{14,10},{16,20},{18,... | collective-permute-start | bytes 811016 | tf_op jit(solution)/shard_map/ppermute | solution.py:527
  51.6 0.1 collective-permute-start.3
  51.7 0.0 all-to-all-done.1
  51.7 7.5 %block_slots.1 = s16[1280,256]{1,0:T(8,128)(2,1)} custom-call(bf16[1280,256]{1,0:T(8,128)(2,1)S(1)} %bitcast.18, s32[256,256]{1,0:T(8,128)S(1)} %positives.1.bits_ref, s32[1,16]{1,0:T(1,128)S(1)} %copy-done.3, s32[1,16]{1,0:T(1,128)S(1)} %copy-done.4, s32[1,16]{1,0:T(1,128)S(1)} %copy-done.5), custom_call_target="tpu_custom_call" | custom-call | flops 34500001792 | tf_op jit(solution)/shard_map/block_slots/pallas_call | solution.py:252
  59.3 0.0 collective-permute-done.1.in1
  59.3 3.7 %collective-permute-done.2.in2 = s16[528,256]{1,0:T(8,128)(2,1)S(1)} collective-permute-done((s16[528,256]{1,0:T(8,128)(2,1)}, s16[528,256]{1,0:T(8,128)(2,1)S(1)}, u32[]{:S(2)}, u32[]{:S(2)}) %collective-permute-start.2) | collective-permute-done | bytes 270368 | tf_op jit(solution)/shard_map/ppermute | solution.py:527
  63.0 0.0 collective-permute-done.3.in3
  63.0 0.7 sum_plane.1
  63.7 1.5 %collective-permute-start.4 = (s16[144,256]{1,0:T(8,128)(2,1)S(1)}, s16[144,256]{1,0:T(8,128)(2,1)S(1)}, u32[]{:S(2)}, u32[]{:S(2)}) collective-permute-start(s16[144,256]{1,0:T(8,128)(2,1)S(1)} %get-tuple-element.42), channel_id=1, source_target_pairs={{0,8},{2,10},{4,12},{6,14},{8,0},{10,2},{12,4},{14,6},{16,24},{18,... | collective-permute-start | bytes 221192 | tf_op jit(solution)/shard_map/ppermute | solution.py:527
  65.2 2.4 %collective-permute-start.5 = (s16[144,256]{1,0:T(8,128)(2,1)S(1)}, s16[144,256]{1,0:T(8,128)(2,1)S(1)}, u32[]{:S(2)}, u32[]{:S(2)}) collective-permute-start(s16[144,256]{1,0:T(8,128)(2,1)S(1)} %get-tuple-element.43), channel_id=1, source_target_pairs={{0,16},{2,18},{4,20},{6,22},{8,24},{10,26},{12,28},{14,30},{16,0},... | collective-permute-start | bytes 221192 | tf_op jit(solution)/shard_map/ppermute | solution.py:527
  67.6 0.6 collective-permute-start.6
  68.2 5.6 %all-to-all-start.2 = ((s16[16,80,256]{2,1,0:T(8,128)(2,1)}), s16[16,80,256]{2,1,0:T(8,128)(2,1)S(1)}, u32[]{:S(2)}, u32[]{:S(2)}) async-start(s16[16,80,256]{2,1,0:T(8,128)(2,1)} %bitcast.12), calls=%async_computation.2 | async-start | bytes 1310720 | tf_op jit(solution)/shard_map/all_to_all | solution.py:530
  73.7 0.0 collective-permute-done.5.in2
  73.7 0.0 collective-permute-done.6.in3
  73.8 0.0 copy-start.1
  73.8 0.3 sum_line.1
  74.1 2.0 %collective-permute-start.7 = (s16[144,256]{1,0:T(8,128)(2,1)S(1)}, s16[144,256]{1,0:T(8,128)(2,1)S(1)}, u32[]{:S(2)}, u32[]{:S(2)}) collective-permute-start(s16[144,256]{1,0:T(8,128)(2,1)S(1)} %sum_line.1), channel_id=1, source_target_pairs={{0,8},{2,10},{4,12},{6,14},{8,0},{10,2},{12,4},{14,6},{16,24},{18,... | collective-permute-start | bytes 221192 | tf_op jit(solution)/shard_map/ppermute | solution.py:527
  76.1 2.4 %collective-permute-start.8 = (s16[144,256]{1,0:T(8,128)(2,1)S(1)}, s16[144,256]{1,0:T(8,128)(2,1)S(1)}, u32[]{:S(2)}, u32[]{:S(2)}) collective-permute-start(s16[144,256]{1,0:T(8,128)(2,1)S(1)} %sum_line.1), channel_id=1, source_target_pairs={{0,16},{2,18},{4,20},{6,22},{8,24},{10,26},{12,28},{14,30},{16,0},... | collective-permute-start | bytes 221192 | tf_op jit(solution)/shard_map/ppermute | solution.py:527
  78.4 0.1 collective-permute-start.9
  78.6 8.5 %collective-permute-done.7 = s16[144,256]{1,0:T(8,128)(2,1)S(1)} collective-permute-done((s16[144,256]{1,0:T(8,128)(2,1)S(1)}, s16[144,256]{1,0:T(8,128)(2,1)S(1)}, u32[]{:S(2)}, u32[]{:S(2)}) %collective-permute-start.7) | collective-permute-done | bytes 73760 | tf_op jit(solution)/shard_map/ppermute | solution.py:527
  87.1 10.0 %collective-permute-done.8 = s16[144,256]{1,0:T(8,128)(2,1)S(1)} collective-permute-done((s16[144,256]{1,0:T(8,128)(2,1)S(1)}, s16[144,256]{1,0:T(8,128)(2,1)S(1)}, u32[]{:S(2)}, u32[]{:S(2)}) %collective-permute-start.8) | collective-permute-done | bytes 73760 | tf_op jit(solution)/shard_map/ppermute | solution.py:527
  97.1 0.0 collective-permute-done.9
  97.1 0.0 all-to-all-done.2
  97.1 0.1 collective-permute-start.10
  97.2 0.5 collective-permute-start
  97.7 1.5 %collective-permute-start.12 = (s16[576,256]{1,0:T(8,128)(2,1)S(1)}, s16[576,256]{1,0:T(8,128)(2,1)S(1)}, u32[]{:S(2)}, u32[]{:S(2)}) collective-permute-start(s16[576,256]{1,0:T(8,128)(2,1)S(1)} %pad_add_fusion.refs_0_), channel_id=1, source_target_pairs={{0,2},{2,0},{4,6},{6,4},{8,10},{10,8},{12,14},{14,12},{16,18},{18,... | collective-permute-start | bytes 884744 | tf_op jit(solution)/shard_map/ppermute | solution.py:527
  99.2 1.5 %collective-permute-start.13 = (s16[576,256]{1,0:T(8,128)(2,1)S(1)}, s16[576,256]{1,0:T(8,128)(2,1)S(1)}, u32[]{:S(2)}, u32[]{:S(2)}) collective-permute-start(s16[576,256]{1,0:T(8,128)(2,1)S(1)} %pad_add_fusion.refs_0_), channel_id=1, source_target_pairs={{0,4},{2,6},{4,0},{6,2},{8,12},{10,14},{12,8},{14,10},{16,20},{18,... | collective-permute-start | bytes 884744 | tf_op jit(solution)/shard_map/ppermute | solution.py:527
  100.6 0.0 collective-permute-done.refs_1_
  100.6 1.0 collective-permute-start.14
  101.7 1.6 %copy-done.6 = f32[2048,256]{1,0:T(8,128)S(1)} copy-done((f32[2048,256]{1,0:T(8,128)S(1)}, f32[2048,256]{1,0:T(8,128)}, u32[]{:S(2)}) %copy-start.6) | copy-done | bytes 2097176
  103.3 5.2 %owner_sums.1 = (f32[2048,256]{1,0:T(8,128)}, f32[1024,256]{1,0:T(8,128)}, f32[32,256]{1,0:T(8,128)}) custom-call(s32[1]{0:T(128)} %bitcast.n_ref, s32[16,128]{1,0:T(8,128)S(1)} %bitcast.21, s32[16,128]{1,0:T(8,128)S(1)} %collective-permute-done.refs_1_, s16[1280,256]{1,0:T(8,128)(2,1)S(1)} %bitcast.17, ...), custom_call_target="tpu_custom_call" | custom-call | flops 34500001792 | tf_op jit(solution)/shard_map/owner_sums/pallas_call | solution.py:496
  108.4 0.0 collective-permute-done.12.refs_1_
  108.4 5.8 %collective-permute-done.13.refs_2_ = s16[576,256]{1,0:T(8,128)(2,1)S(1)} collective-permute-done((s16[576,256]{1,0:T(8,128)(2,1)S(1)}, s16[576,256]{1,0:T(8,128)(2,1)S(1)}, u32[]{:S(2)}, u32[]{:S(2)}) %collective-permute-start.13) | collective-permute-done | bytes 294944 | tf_op jit(solution)/shard_map/ppermute | solution.py:527
  114.2 1.9 %decode_features.1 = f32[2048,256]{1,0:T(8,128)} custom-call(s32[1]{0:T(128)} %bitcast.11.w_ref, s16[576,256]{1,0:T(8,128)(2,1)S(1)} %pad_add_fusion.refs_0_, s16[576,256]{1,0:T(8,128)(2,1)S(1)} %collective-permute-done.12.refs_1_, s16[576,256]{1,0:T(8,128)(2,1)S(1)} %collective-permute-done.13.refs_2_, s16[576,256]{1,0:T(8,128)(2,1)S(1)} %collective-permute-done.14.refs_3_), custom_call_target="tpu_custom_call" | custom-call | flops 1048576 | bytes 3145728 | tf_op jit(solution)/shard_map/decode_features/pallas_call | solution.py:414
  (14 shorter events, 0.0 us)
Async XLA Ops:
  2.1 15.5 %all-to-all-start = ((s32[16,1,128]{2,1,0:T(1,128)}), s32[16,1,128]{2,1,0:T(1,128)S(1)}, u32[]{:S(2)}, u32[]{:S(2)}) async-start(s32[16,1,128]{2,1,0:T(1,128)} %bitcast.24), calls=%async_computation | async-start | bytes 16384 | tf_op jit(solution)/shard_map/all_to_all | solution.py:530
  10.4 0.7 copy-start.2
  17.6 0.6 copy-start
  23.0 28.7 %all-to-all-start.1 = ((bf16[16,80,256]{2,1,0:T(8,128)(2,1)}), bf16[16,80,256]{2,1,0:T(8,128)(2,1)S(1)}, u32[]{:S(2)}, u32[]{:S(2)}) async-start(bf16[16,80,256]{2,1,0:T(8,128)(2,1)} %bitcast.23), calls=%async_computation.1 | async-start | bytes 1310720 | tf_op jit(solution)/shard_map/all_to_all | solution.py:530
  28.2 23.5 %copy-start.3 = (s32[1,16]{1,0:T(1,128)S(1)}, s32[1,16]{1,0:T(1,128)}, u32[]{:S(2)}) copy-start(s32[1,16]{1,0:T(1,128)} %uc_ref.1) | copy-start | bytes 196
  28.2 23.5 %copy-start.4 = (s32[1,16]{1,0:T(1,128)S(1)}, s32[1,16]{1,0:T(1,128)}, u32[]{:S(2)}) copy-start(s32[1,16]{1,0:T(1,128)} %vc_ref.1) | copy-start | bytes 196
  28.2 23.5 %copy-start.5 = (s32[1,16]{1,0:T(1,128)S(1)}, s32[1,16]{1,0:T(1,128)}, u32[]{:S(2)}) copy-start(s32[1,16]{1,0:T(1,128)} %wc_ref.1) | copy-start | bytes 196
  48.2 11.1 %collective-permute-start.1 = (s16[528,256]{1,0:T(8,128)(2,1)}, s16[528,256]{1,0:T(8,128)(2,1)S(1)}, u32[]{:S(2)}, u32[]{:S(2)}) collective-permute-start(s16[528,256]{1,0:T(8,128)(2,1)} %get-tuple-element.38), channel_id=1, source_target_pairs={{0,2},{2,0},{4,6},{6,4},{8,10},{10,8},{12,14},{14,12},{16,18},{18,... | collective-permute-start | bytes 811016 | tf_op jit(solution)/shard_map/ppermute | solution.py:527
  50.1 12.8 %collective-permute-start.2 = (s16[528,256]{1,0:T(8,128)(2,1)}, s16[528,256]{1,0:T(8,128)(2,1)S(1)}, u32[]{:S(2)}, u32[]{:S(2)}) collective-permute-start(s16[528,256]{1,0:T(8,128)(2,1)} %get-tuple-element.39), channel_id=1, source_target_pairs={{0,4},{2,6},{4,0},{6,2},{8,12},{10,14},{12,8},{14,10},{16,20},{18,... | collective-permute-start | bytes 811016 | tf_op jit(solution)/shard_map/ppermute | solution.py:527
  51.6 11.4 %collective-permute-start.3 = (s16[528,256]{1,0:T(8,128)(2,1)}, s16[528,256]{1,0:T(8,128)(2,1)S(1)}, u32[]{:S(2)}, u32[]{:S(2)}) collective-permute-start(s16[528,256]{1,0:T(8,128)(2,1)} %get-tuple-element.40), channel_id=1, source_target_pairs={{0,6},{2,4},{4,2},{6,0},{8,14},{10,12},{12,10},{14,8},{16,22},{18,... | collective-permute-start | bytes 811016 | tf_op jit(solution)/shard_map/ppermute | solution.py:527
  51.7 11.2 %copy-start.7 = (f32[512,256]{1,0:T(8,128)S(1)}, f32[512,256]{1,0:T(8,128)}, u32[]{:S(2)}) copy-start(f32[512,256]{1,0:T(8,128)} %get-tuple-element.37.own_ref) | copy-start | bytes 1572868
  63.7 10.0 %collective-permute-start.4 = (s16[144,256]{1,0:T(8,128)(2,1)S(1)}, s16[144,256]{1,0:T(8,128)(2,1)S(1)}, u32[]{:S(2)}, u32[]{:S(2)}) collective-permute-start(s16[144,256]{1,0:T(8,128)(2,1)S(1)} %get-tuple-element.42), channel_id=1, source_target_pairs={{0,8},{2,10},{4,12},{6,14},{8,0},{10,2},{12,4},{14,6},{16,24},{18,... | collective-permute-start | bytes 221192 | tf_op jit(solution)/shard_map/ppermute | solution.py:527
  65.2 8.5 %collective-permute-start.5 = (s16[144,256]{1,0:T(8,128)(2,1)S(1)}, s16[144,256]{1,0:T(8,128)(2,1)S(1)}, u32[]{:S(2)}, u32[]{:S(2)}) collective-permute-start(s16[144,256]{1,0:T(8,128)(2,1)S(1)} %get-tuple-element.43), channel_id=1, source_target_pairs={{0,16},{2,18},{4,20},{6,22},{8,24},{10,26},{12,28},{14,30},{16,0},... | collective-permute-start | bytes 221192 | tf_op jit(solution)/shard_map/ppermute | solution.py:527
  67.6 6.2 %collective-permute-start.6 = (s16[144,256]{1,0:T(8,128)(2,1)S(1)}, s16[144,256]{1,0:T(8,128)(2,1)S(1)}, u32[]{:S(2)}, u32[]{:S(2)}) collective-permute-start(s16[144,256]{1,0:T(8,128)(2,1)S(1)} %get-tuple-element.44), channel_id=1, source_target_pairs={{0,24},{2,26},{4,28},{6,30},{8,16},{10,18},{12,20},{14,22},{16,8},... | collective-permute-start | bytes 221192 | tf_op jit(solution)/shard_map/ppermute | solution.py:527
  68.2 33.5 %collective-permute-start.11 = (f32[2048,256]{1,0:T(8,128)}, f32[2048,256]{1,0:T(8,128)S(1)}, u32[]{:S(2)}, u32[]{:S(2)}) collective-permute-start(f32[2048,256]{1,0:T(8,128)} %get-tuple-element.47), channel_id=1, source_target_pairs={{0,1},{1,0},{2,3},{3,2},{4,5},{5,4},{6,7},{7,6},{8,9},{9,8},{10,11... | collective-permute-start | bytes 6291464 | tf_op jit(solution)/shard_map/ppermute | solution.py:533
  68.2 28.9 %all-to-all-start.2 = ((s16[16,80,256]{2,1,0:T(8,128)(2,1)}), s16[16,80,256]{2,1,0:T(8,128)(2,1)S(1)}, u32[]{:S(2)}, u32[]{:S(2)}) async-start(s16[16,80,256]{2,1,0:T(8,128)(2,1)} %bitcast.12), calls=%async_computation.2 | async-start | bytes 1310720 | tf_op jit(solution)/shard_map/all_to_all | solution.py:530
  73.8 23.4 %copy-start.1 = (s32[16,1,128]{2,1,0:T(1,128)S(1)}, s32[16,1,128]{2,1,0:T(1,128)}, u32[]{:S(2)}) copy-start(s32[16,1,128]{2,1,0:T(1,128)} %copy-done) | copy-start | bytes 24580
  74.1 13.0 %collective-permute-start.7 = (s16[144,256]{1,0:T(8,128)(2,1)S(1)}, s16[144,256]{1,0:T(8,128)(2,1)S(1)}, u32[]{:S(2)}, u32[]{:S(2)}) collective-permute-start(s16[144,256]{1,0:T(8,128)(2,1)S(1)} %sum_line.1), channel_id=1, source_target_pairs={{0,8},{2,10},{4,12},{6,14},{8,0},{10,2},{12,4},{14,6},{16,24},{18,... | collective-permute-start | bytes 221192 | tf_op jit(solution)/shard_map/ppermute | solution.py:527
  76.1 21.0 %collective-permute-start.8 = (s16[144,256]{1,0:T(8,128)(2,1)S(1)}, s16[144,256]{1,0:T(8,128)(2,1)S(1)}, u32[]{:S(2)}, u32[]{:S(2)}) collective-permute-start(s16[144,256]{1,0:T(8,128)(2,1)S(1)} %sum_line.1), channel_id=1, source_target_pairs={{0,16},{2,18},{4,20},{6,22},{8,24},{10,26},{12,28},{14,30},{16,0},... | collective-permute-start | bytes 221192 | tf_op jit(solution)/shard_map/ppermute | solution.py:527
  78.4 18.6 %collective-permute-start.9 = (s16[144,256]{1,0:T(8,128)(2,1)S(1)}, s16[144,256]{1,0:T(8,128)(2,1)S(1)}, u32[]{:S(2)}, u32[]{:S(2)}) collective-permute-start(s16[144,256]{1,0:T(8,128)(2,1)S(1)} %sum_line.1), channel_id=1, source_target_pairs={{0,24},{2,26},{4,28},{6,30},{8,16},{10,18},{12,20},{14,22},{16,8},... | collective-permute-start | bytes 221192 | tf_op jit(solution)/shard_map/ppermute | solution.py:527
  97.1 4.5 %collective-permute-start.10 = (s16[1280,256]{1,0:T(8,128)(2,1)S(1)}, s16[1280,256]{1,0:T(8,128)(2,1)S(1)}, u32[]{:S(2)}, u32[]{:S(2)}) collective-permute-start(s16[1280,256]{1,0:T(8,128)(2,1)S(1)} %bitcast.16), channel_id=1, source_target_pairs={{0,1},{1,0},{2,3},{3,2},{4,5},{5,4},{6,7},{7,6},{8,9},{9,8},{10,11... | collective-permute-start | bytes 1966088 | tf_op jit(solution)/shard_map/ppermute | solution.py:533
  97.2 3.4 %collective-permute-start = (s32[16,128]{1,0:T(8,128)S(1)}, s32[16,128]{1,0:T(8,128)S(1)}, u32[]{:S(2)}, u32[]{:S(2)}) collective-permute-start(s32[16,128]{1,0:T(8,128)S(1)} %bitcast.20), channel_id=1, source_target_pairs={{0,1},{1,0},{2,3},{3,2},{4,5},{5,4},{6,7},{7,6},{8,9},{9,8},{10,11... | collective-permute-start | bytes 24584 | tf_op jit(solution)/shard_map/ppermute | solution.py:533
  97.7 10.8 %collective-permute-start.12 = (s16[576,256]{1,0:T(8,128)(2,1)S(1)}, s16[576,256]{1,0:T(8,128)(2,1)S(1)}, u32[]{:S(2)}, u32[]{:S(2)}) collective-permute-start(s16[576,256]{1,0:T(8,128)(2,1)S(1)} %pad_add_fusion.refs_0_), channel_id=1, source_target_pairs={{0,2},{2,0},{4,6},{6,4},{8,10},{10,8},{12,14},{14,12},{16,18},{18,... | collective-permute-start | bytes 884744 | tf_op jit(solution)/shard_map/ppermute | solution.py:527
  99.2 15.0 %collective-permute-start.13 = (s16[576,256]{1,0:T(8,128)(2,1)S(1)}, s16[576,256]{1,0:T(8,128)(2,1)S(1)}, u32[]{:S(2)}, u32[]{:S(2)}) collective-permute-start(s16[576,256]{1,0:T(8,128)(2,1)S(1)} %pad_add_fusion.refs_0_), channel_id=1, source_target_pairs={{0,4},{2,6},{4,0},{6,2},{8,12},{10,14},{12,8},{14,10},{16,20},{18,... | collective-permute-start | bytes 884744 | tf_op jit(solution)/shard_map/ppermute | solution.py:527
  100.6 13.6 %collective-permute-start.14 = (s16[576,256]{1,0:T(8,128)(2,1)S(1)}, s16[576,256]{1,0:T(8,128)(2,1)S(1)}, u32[]{:S(2)}, u32[]{:S(2)}) collective-permute-start(s16[576,256]{1,0:T(8,128)(2,1)S(1)} %pad_add_fusion.refs_0_), channel_id=1, source_target_pairs={{0,6},{2,4},{4,2},{6,0},{8,14},{10,12},{12,10},{14,8},{16,22},{18,... | collective-permute-start | bytes 884744 | tf_op jit(solution)/shard_map/ppermute | solution.py:527
  101.7 1.6 %copy-start.6 = (f32[2048,256]{1,0:T(8,128)S(1)}, f32[2048,256]{1,0:T(8,128)}, u32[]{:S(2)}) copy-start(f32[2048,256]{1,0:T(8,128)} %get-tuple-element.46.refs_4_) | copy-start | bytes 6291460

commit v3 on v2

--- a/solution.py
+++ b/solution.py
@@ -261,7 +261,7 @@
     )(back, bits, uc, vc, wc)
 
 
-def dense_kernel(shares, per, chunk, n_ref, w_ref, x_ref, u_ref, f_ref, others_ref, mine_ref, own_ref, g1, g2, g3, acc, ft):
+def dense_kernel(shares, per, chunk, n_ref, w_ref, x_ref, u_ref, f_ref, others_ref, mine_ref, own_ref, g1, g2, g3, acc):
     t = pl.program_id(0)
     u = u_ref[...]
     nf = f_ref.shape[0]
@@ -269,12 +269,11 @@
     @pl.when(t == 0)
     def _():
         acc[...] = jnp.zeros_like(acc)
-        ft[...] = f_ref[...].astype(F32).T.astype(BF16)
 
     total = None
     for c in range(0, nf, chunk):
         f = f_ref[c : c + chunk, :]
-        r = (mm(u, ft[:, c : c + chunk]) - x_ref[:, c : c + chunk].astype(F32)).astype(BF16)
+        r = (mm(u, f, NT) - x_ref[:, c : c + chunk].astype(F32)).astype(BF16)
         part = mm(r, f)
         total = part if total is None else total + part
         acc[c : c + chunk, :] += mm(r, u, TN)
@@ -350,7 +349,7 @@
                 pl.BlockSpec((nf // PLANE, RANK), lambda t, n_ref, w_ref: (0, 0)),
             ]
             + [pl.BlockSpec((nf // PLANE + TAIL, RANK), lambda t, n_ref, w_ref: (0, 0))] * 3,
-            scratch_shapes=[pltpu.VMEM((nf, RANK), F32), pltpu.VMEM((RANK, nf), BF16)],
+            scratch_shapes=[pltpu.VMEM((nf, RANK), F32)],
         ),
         out_shape=[
             jax.ShapeDtypeStruct(((shares - 1) * own, RANK), F32),
@@ -499,7 +498,7 @@
         out_specs=[VM] * 3,
         out_shape=[jax.ShapeDtypeStruct((r, RANK), F32) for r in (own_u, own_i, own_w)],
         compiler_params=params(28),
-        cost_estimate=busy(30),
+        cost_estimate=busy(1),
         name="owner_sums",
     )(n, *gots, *rets, *parts)
 
@@ -545,11 +544,12 @@
     packed = [flip(x, m + 1) for m, x in enumerate(packed)]
     own, slots = tie((own, slots))
     own, *packed = sum_plane(w, own, packed)
-    ret = across(slots)
     mark = sum_line(own, [flip(x, PLANE * (m + 1)) for m, x in enumerate(packed)])
     known = jnp.concatenate([mark] + [flip(mark, PLANE * m) for m in range(1, 4)], axis=0)
-    ret, known = tie((ret, known))
+    slots, known = tie((slots, known))
     knowns = [known] + [flip(known, m) for m in range(1, PLANE)]
+    ret = across(slots)
+    ret, knowns[1], knowns[2] = tie((ret, knowns[1], knowns[2]))
     gots = [got] + [shift(got, r) for r in range(1, shares)]
     rets = [ret] + [shift(ret, r) for r in range(1, shares)]
     parts = [mine] + [shift(others[own_u * (r - 1) : own_u * r], r) for r in range(1, shares)]

time: 117 us -> 112 us (0.957)
  waiting for transfers between devices: 29.8 us -> 25.9 us
    ppermute x12, waiting for transfers between devices: 28 us -> 22.3 us  [flip(): return lax.ppermute(x, 'wide', [(i, i ^ bits) for i in range(owners)])]
    pallas_call x1, Pallas kernels: 5.19 us -> 6.76 us  [owner_sums(): pl.pallas_call(functools.partial(owner_kernel, shares), in_specs=[SM] + [...]
    unnamed x16 -> x22, local copies, waits for them, and re-layouts: 2.93 us -> 2.06 us
  transfers between devices with their start and end apart: 18 -> 18, of which waited for: 5 -> 12; matrix products, arithmetic and copies ran while one was open for 0% -> 0% of each run, Pallas kernels for 32% -> 34%
where the time goes in v3:
time: 112 us
  Pallas kernels  47.2 us (42%)
  starting transfers between devices  36 us (32%)
  waiting for transfers between devices  25.9 us (23%)
  local copies, waits for them, and re-layouts  2.06 us (2%)
    ppermute x12, waiting for transfers between devices, flip(): return lax.ppermute(x, 'wide', [(i, i ^ bits) for i in range(owners)])  22.3 us
    pallas_call x1, Pallas kernels, dense(): pl.pallas_call(functools.partial(dense_kernel, shares, per, nf), grid_spe...  19.8 us
    all_to_all x3, starting transfers between devices, across(): return lax.all_to_all(x, 'wide', split_axis=0, concat_axis=0, tiled=True)  18.6 us
    ppermute x12, starting transfers between devices, flip(): return lax.ppermute(x, 'wide', [(i, i ^ bits) for i in range(owners)])  17.1 us
    pallas_call x1, Pallas kernels, owner_sums(): pl.pallas_call(functools.partial(owner_kernel, shares), in_specs=[SM] + [...  6.76 us
    pallas_call x1, Pallas kernels, block_slots(): pl.pallas_call(functools.partial(block_kernel, owners), in_specs=[VM, VM,...  6.7 us
    pallas_call x1, Pallas kernels, gather_rows(): pl.pallas_call(functools.partial(gather_kernel, owners), in_specs=[VM] *...  4.84 us
    pallas_call x1, Pallas kernels, positives(): pl.pallas_call(positives_kernel, in_specs=[VM], out_specs=VM, out_shape=j...  4.69 us
  transfers between devices with their start and end apart: 18, of which 12 were waited for; matrix products, arithmetic and copies ran while one was open for 0% of the time, Pallas kernels for 34%

profile of v3, /device:TPU:0, one launch (start us, length us, event | category | flops | bytes accessed | tf_op | source)
XLA Modules:
  0.0 112.0 jit_solution(15207267182290294010)
XLA Ops:
  0.6 1.5 %requests.1 = s32[16,128]{1,0:T(8,128)} custom-call(s32[16,32]{1,0:T(8,128)} %bitcast.26, s32[16,32]{1,0:T(8,128)} %bitcast.27, s32[4,16]{1,0:T(4,128)} %bitcast.28), custom_call_target="tpu_custom_call" | custom-call | tf_op jit(solution)/shard_map/requests/pallas_call | solution.py:75
  2.1 8.3 %all-to-all-start = ((s32[16,1,128]{2,1,0:T(1,128)}), s32[16,1,128]{2,1,0:T(1,128)S(1)}, u32[]{:S(2)}, u32[]{:S(2)}) async-start(s32[16,1,128]{2,1,0:T(1,128)} %bitcast.25), calls=%async_computation | async-start | bytes 16384 | tf_op jit(solution)/shard_map/all_to_all | solution.py:529
  10.4 0.0 copy-start.6
  10.4 0.7 copy-done.6
  11.1 4.7 %positives.1.bits_ref = s32[256,256]{1,0:T(8,128)S(1)} custom-call(s32[32,128]{1,0:T(8,128)S(1)} %bitcast.23), custom_call_target="tpu_custom_call" | custom-call | flops 6899999744 | tf_op jit(solution)/shard_map/positives/pallas_call | solution.py:157
  15.8 1.8 %all-to-all-done = s32[16,1,128]{2,1,0:T(1,128)S(1)} async-done(((s32[16,1,128]{2,1,0:T(1,128)}), s32[16,1,128]{2,1,0:T(1,128)S(1)}, u32[]{:S(2)}, u32[]{:S(2)}) %all-to-all-start) | async-done | bytes 8224 | tf_op jit(solution)/shard_map/all_to_all | solution.py:529
  17.6 0.6 copy-done.4
  18.2 4.8 %gather_rows.1 = bf16[1280,256]{1,0:T(8,128)(2,1)} custom-call(s32[16,128]{1,0:T(8,128)} %bitcast.20, bf16[4096,256]{1,0:T(8,128)(2,1)} %u_ref.1, bf16[2048,256]{1,0:T(8,128)(2,1)} %it_ref.1, bf16[64,256]{1,0:T(8,128)(2,1)} %wt_ref.1), custom_call_target="tpu_custom_call" | custom-call | flops 5750000128 | tf_op jit(solution)/shard_map/gather_rows/pallas_call | solution.py:112
  23.0 5.2 %all-to-all-start.1 = ((bf16[16,80,256]{2,1,0:T(8,128)(2,1)}), bf16[16,80,256]{2,1,0:T(8,128)(2,1)S(1)}, u32[]{:S(2)}, u32[]{:S(2)}) async-start(bf16[16,80,256]{2,1,0:T(8,128)(2,1)} %bitcast.24), calls=%async_computation.1 | async-start | bytes 1310720 | tf_op jit(solution)/shard_map/all_to_all | solution.py:529
  28.2 0.0 copy-start.7
  28.2 0.0 copy-start.8
  28.2 0.0 copy-start.9
  28.3 19.8 %dense.1 = (f32[2048,256]{1,0:T(8,128)}, f32[2048,256]{1,0:T(8,128)}, f32[512,256]{1,0:T(8,128)}, s16[528,256]{1,0:T(8,128)(2,1)}, s16[528,256]{1,0:T(8,128)(2,1)}, /*index=5*/s16[528,256]{1,0:T(8,128)(2,1)}) custom-call(s32[1]{0:T(128)} %bitcast.n_ref, s32[1]{0:T(128)} %bitcast.11.w_ref, bf16[4096,2048]{1,0:T(8,128)(2,1)} %x_ref.1, ...), custom_call_target="tpu_custom_call" | custom-call | flops 12884901888 | bytes 25165824 | tf_op jit(solution)/shard_map/dense/pallas_call | solution.py:336
  48.0 2.1 %collective-permute-start.1 = (s16[528,256]{1,0:T(8,128)(2,1)}, s16[528,256]{1,0:T(8,128)(2,1)S(1)}, u32[]{:S(2)}, u32[]{:S(2)}) collective-permute-start(s16[528,256]{1,0:T(8,128)(2,1)} %get-tuple-element.41), channel_id=1, source_target_pairs={{0,2},{2,0},{4,6},{6,4},{8,10},{10,8},{12,14},{14,12},{16,18},{18,... | collective-permute-start | bytes 811016 | tf_op jit(solution)/shard_map/ppermute | solution.py:526
  50.1 1.5 %collective-permute-start.2 = (s16[528,256]{1,0:T(8,128)(2,1)}, s16[528,256]{1,0:T(8,128)(2,1)S(1)}, u32[]{:S(2)}, u32[]{:S(2)}) collective-permute-start(s16[528,256]{1,0:T(8,128)(2,1)} %get-tuple-element.42), channel_id=1, source_target_pairs={{0,4},{2,6},{4,0},{6,2},{8,12},{10,14},{12,8},{14,10},{16,20},{18,... | collective-permute-start | bytes 811016 | tf_op jit(solution)/shard_map/ppermute | solution.py:526
  51.6 0.1 collective-permute-start.3
  51.7 0.0 all-to-all-done.1
  51.7 6.7 %block_slots.1 = s16[1280,256]{1,0:T(8,128)(2,1)S(1)} custom-call(bf16[1280,256]{1,0:T(8,128)(2,1)S(1)} %bitcast.19, s32[256,256]{1,0:T(8,128)S(1)} %positives.1.bits_ref, s32[1,16]{1,0:T(1,128)S(1)} %copy-done.7, s32[1,16]{1,0:T(1,128)S(1)} %copy-done.8, s32[1,16]{1,0:T(1,128)S(1)} %copy-done.9), custom_call_target="tpu_custom_call" | custom-call | flops 34500001792 | tf_op jit(solution)/shard_map/block_slots/pallas_call | solution.py:252
  58.4 0.0 copy-start.1
  58.4 0.0 collective-permute-done.1.in1
  58.4 4.5 %collective-permute-done.2.in2 = s16[528,256]{1,0:T(8,128)(2,1)S(1)} collective-permute-done((s16[528,256]{1,0:T(8,128)(2,1)}, s16[528,256]{1,0:T(8,128)(2,1)S(1)}, u32[]{:S(2)}, u32[]{:S(2)}) %collective-permute-start.2) | collective-permute-done | bytes 270368 | tf_op jit(solution)/shard_map/ppermute | solution.py:526
  63.0 0.0 collective-permute-done.3.in3
  63.0 0.7 sum_plane.1
  63.7 1.5 %collective-permute-start.4 = (s16[144,256]{1,0:T(8,128)(2,1)S(1)}, s16[144,256]{1,0:T(8,128)(2,1)S(1)}, u32[]{:S(2)}, u32[]{:S(2)}) collective-permute-start(s16[144,256]{1,0:T(8,128)(2,1)S(1)} %get-tuple-element.45), channel_id=1, source_target_pairs={{0,8},{2,10},{4,12},{6,14},{8,0},{10,2},{12,4},{14,6},{16,24},{18,... | collective-permute-start | bytes 221192 | tf_op jit(solution)/shard_map/ppermute | solution.py:526
  65.2 2.4 %collective-permute-start.5 = (s16[144,256]{1,0:T(8,128)(2,1)S(1)}, s16[144,256]{1,0:T(8,128)(2,1)S(1)}, u32[]{:S(2)}, u32[]{:S(2)}) collective-permute-start(s16[144,256]{1,0:T(8,128)(2,1)S(1)} %get-tuple-element.46), channel_id=1, source_target_pairs={{0,16},{2,18},{4,20},{6,22},{8,24},{10,26},{12,28},{14,30},{16,0},... | collective-permute-start | bytes 221192 | tf_op jit(solution)/shard_map/ppermute | solution.py:526
  67.6 0.6 collective-permute-start.6
  68.1 0.2 collective-permute-done.4.in1
  68.3 3.2 %collective-permute-done.5.in2 = s16[144,256]{1,0:T(8,128)(2,1)S(1)} collective-permute-done((s16[144,256]{1,0:T(8,128)(2,1)S(1)}, s16[144,256]{1,0:T(8,128)(2,1)S(1)}, u32[]{:S(2)}, u32[]{:S(2)}) %collective-permute-start.5) | collective-permute-done | bytes 73760 | tf_op jit(solution)/shard_map/ppermute | solution.py:526
  71.5 2.8 %collective-permute-done.6.in3 = s16[144,256]{1,0:T(8,128)(2,1)S(1)} collective-permute-done((s16[144,256]{1,0:T(8,128)(2,1)S(1)}, s16[144,256]{1,0:T(8,128)(2,1)S(1)}, u32[]{:S(2)}, u32[]{:S(2)}) %collective-permute-start.6) | collective-permute-done | bytes 73760 | tf_op jit(solution)/shard_map/ppermute | solution.py:526
  74.3 0.3 sum_line.1
  74.6 0.1 collective-permute-start.7
  74.7 0.9 collective-permute-start.8
  75.6 3.5 %collective-permute-start.9 = (s16[144,256]{1,0:T(8,128)(2,1)S(1)}, s16[144,256]{1,0:T(8,128)(2,1)S(1)}, u32[]{:S(2)}, u32[]{:S(2)}) collective-permute-start(s16[144,256]{1,0:T(8,128)(2,1)S(1)} %sum_line.1), channel_id=1, source_target_pairs={{0,24},{2,26},{4,28},{6,30},{8,16},{10,18},{12,20},{14,22},{16,8},... | collective-permute-start | bytes 221192 | tf_op jit(solution)/shard_map/ppermute | solution.py:526
  79.1 0.9 collective-permute-done.8
  80.0 2.3 %collective-permute-done.9 = s16[144,256]{1,0:T(8,128)(2,1)S(1)} collective-permute-done((s16[144,256]{1,0:T(8,128)(2,1)S(1)}, s16[144,256]{1,0:T(8,128)(2,1)S(1)}, u32[]{:S(2)}, u32[]{:S(2)}) %collective-permute-start.9) | collective-permute-done | bytes 73760 | tf_op jit(solution)/shard_map/ppermute | solution.py:526
  82.3 5.2 %all-to-all-start.2 = ((s16[16,80,256]{2,1,0:T(8,128)(2,1)}), s16[16,80,256]{2,1,0:T(8,128)(2,1)S(1)}, u32[]{:S(2)}, u32[]{:S(2)}) async-start(s16[16,80,256]{2,1,0:T(8,128)(2,1)} %bitcast.18), calls=%async_computation.2 | async-start | bytes 1310720 | tf_op jit(solution)/shard_map/all_to_all | solution.py:529
  87.5 2.0 %collective-permute-start.10 = (s16[576,256]{1,0:T(8,128)(2,1)S(1)}, s16[576,256]{1,0:T(8,128)(2,1)S(1)}, u32[]{:S(2)}, u32[]{:S(2)}) collective-permute-start(s16[576,256]{1,0:T(8,128)(2,1)S(1)} %pad_add_fusion.refs_0_), channel_id=1, source_target_pairs={{0,2},{2,0},{4,6},{6,4},{8,10},{10,8},{12,14},{14,12},{16,18},{18,... | collective-permute-start | bytes 884744 | tf_op jit(solution)/shard_map/ppermute | solution.py:526
  89.5 1.5 %collective-permute-start.11 = (s16[576,256]{1,0:T(8,128)(2,1)S(1)}, s16[576,256]{1,0:T(8,128)(2,1)S(1)}, u32[]{:S(2)}, u32[]{:S(2)}) collective-permute-start(s16[576,256]{1,0:T(8,128)(2,1)S(1)} %pad_add_fusion.refs_0_), channel_id=1, source_target_pairs={{0,4},{2,6},{4,0},{6,2},{8,12},{10,14},{12,8},{14,10},{16,20},{18,... | collective-permute-start | bytes 884744 | tf_op jit(solution)/shard_map/ppermute | solution.py:526
  90.9 6.7 %collective-permute-done.10.refs_1_ = s16[576,256]{1,0:T(8,128)(2,1)S(1)} collective-permute-done((s16[576,256]{1,0:T(8,128)(2,1)S(1)}, s16[576,256]{1,0:T(8,128)(2,1)S(1)}, u32[]{:S(2)}, u32[]{:S(2)}) %collective-permute-start.10) | collective-permute-done | bytes 294944 | tf_op jit(solution)/shard_map/ppermute | solution.py:526
  97.7 0.5 collective-permute-done.11.refs_2_
  98.1 0.7 copy-done.2
  98.8 0.9 all-to-all-done.2
  99.8 1.2 %collective-permute-start.14 = (s16[576,256]{1,0:T(8,128)(2,1)S(1)}, s16[576,256]{1,0:T(8,128)(2,1)S(1)}, u32[]{:S(2)}, u32[]{:S(2)}) collective-permute-start(s16[576,256]{1,0:T(8,128)(2,1)S(1)} %pad_add_fusion.refs_0_), channel_id=1, source_target_pairs={{0,6},{2,4},{4,2},{6,0},{8,14},{10,12},{12,10},{14,8},{16,22},{18,... | collective-permute-start | bytes 884744 | tf_op jit(solution)/shard_map/ppermute | solution.py:526
  100.9 0.2 collective-permute-start
  101.2 0.9 collective-permute-done.refs_1_
  102.1 6.8 %owner_sums.1 = (f32[2048,256]{1,0:T(8,128)}, f32[1024,256]{1,0:T(8,128)}, f32[32,256]{1,0:T(8,128)}) custom-call(s32[1]{0:T(128)} %bitcast.n_ref, s32[16,128]{1,0:T(8,128)S(1)} %bitcast.22, s32[16,128]{1,0:T(8,128)S(1)} %collective-permute-done.refs_1_, s16[1280,256]{1,0:T(8,128)(2,1)S(1)} %bitcast.17, ...), custom_call_target="tpu_custom_call" | custom-call | flops 1150000000 | tf_op jit(solution)/shard_map/owner_sums/pallas_call | solution.py:495
  108.9 1.2 %collective-permute-done.14.refs_3_ = s16[576,256]{1,0:T(8,128)(2,1)S(1)} collective-permute-done((s16[576,256]{1,0:T(8,128)(2,1)S(1)}, s16[576,256]{1,0:T(8,128)(2,1)S(1)}, u32[]{:S(2)}, u32[]{:S(2)}) %collective-permute-start.14) | collective-permute-done | bytes 294944 | tf_op jit(solution)/shard_map/ppermute | solution.py:526
  110.1 1.9 %decode_features.1 = f32[2048,256]{1,0:T(8,128)} custom-call(s32[1]{0:T(128)} %bitcast.11.w_ref, s16[576,256]{1,0:T(8,128)(2,1)S(1)} %pad_add_fusion.refs_0_, s16[576,256]{1,0:T(8,128)(2,1)S(1)} %collective-permute-done.10.refs_1_, s16[576,256]{1,0:T(8,128)(2,1)S(1)} %copy-done.3, s16[576,256]{1,0:T(8,128)(2,1)S(1)} %collective-permute-done.14.refs_3_), custom_call_target="tpu_custom_call" | custom-call | flops 1048576 | bytes 3145728 | tf_op jit(solution)/shard_map/decode_features/pallas_call | solution.py:413
  (20 shorter events, 0.1 us)
Async XLA Ops:
  2.1 15.5 %all-to-all-start = ((s32[16,1,128]{2,1,0:T(1,128)}), s32[16,1,128]{2,1,0:T(1,128)S(1)}, u32[]{:S(2)}, u32[]{:S(2)}) async-start(s32[16,1,128]{2,1,0:T(1,128)} %bitcast.25), calls=%async_computation | async-start | bytes 16384 | tf_op jit(solution)/shard_map/all_to_all | solution.py:529
  10.4 0.7 copy-start.6
  17.6 0.6 copy-start.4
  23.0 28.6 %all-to-all-start.1 = ((bf16[16,80,256]{2,1,0:T(8,128)(2,1)}), bf16[16,80,256]{2,1,0:T(8,128)(2,1)S(1)}, u32[]{:S(2)}, u32[]{:S(2)}) async-start(bf16[16,80,256]{2,1,0:T(8,128)(2,1)} %bitcast.24), calls=%async_computation.1 | async-start | bytes 1310720 | tf_op jit(solution)/shard_map/all_to_all | solution.py:529
  28.2 23.4 %copy-start.7 = (s32[1,16]{1,0:T(1,128)S(1)}, s32[1,16]{1,0:T(1,128)}, u32[]{:S(2)}) copy-start(s32[1,16]{1,0:T(1,128)} %uc_ref.1) | copy-start | bytes 196
  28.2 23.4 %copy-start.8 = (s32[1,16]{1,0:T(1,128)S(1)}, s32[1,16]{1,0:T(1,128)}, u32[]{:S(2)}) copy-start(s32[1,16]{1,0:T(1,128)} %vc_ref.1) | copy-start | bytes 196
  28.2 23.4 %copy-start.9 = (s32[1,16]{1,0:T(1,128)S(1)}, s32[1,16]{1,0:T(1,128)}, u32[]{:S(2)}) copy-start(s32[1,16]{1,0:T(1,128)} %wc_ref.1) | copy-start | bytes 196
  48.0 10.4 %collective-permute-start.1 = (s16[528,256]{1,0:T(8,128)(2,1)}, s16[528,256]{1,0:T(8,128)(2,1)S(1)}, u32[]{:S(2)}, u32[]{:S(2)}) collective-permute-start(s16[528,256]{1,0:T(8,128)(2,1)} %get-tuple-element.41), channel_id=1, source_target_pairs={{0,2},{2,0},{4,6},{6,4},{8,10},{10,8},{12,14},{14,12},{16,18},{18,... | collective-permute-start | bytes 811016 | tf_op jit(solution)/shard_map/ppermute | solution.py:526
  50.1 12.8 %collective-permute-start.2 = (s16[528,256]{1,0:T(8,128)(2,1)}, s16[528,256]{1,0:T(8,128)(2,1)S(1)}, u32[]{:S(2)}, u32[]{:S(2)}) collective-permute-start(s16[528,256]{1,0:T(8,128)(2,1)} %get-tuple-element.42), channel_id=1, source_target_pairs={{0,4},{2,6},{4,0},{6,2},{8,12},{10,14},{12,8},{14,10},{16,20},{18,... | collective-permute-start | bytes 811016 | tf_op jit(solution)/shard_map/ppermute | solution.py:526
  51.6 11.4 %collective-permute-start.3 = (s16[528,256]{1,0:T(8,128)(2,1)}, s16[528,256]{1,0:T(8,128)(2,1)S(1)}, u32[]{:S(2)}, u32[]{:S(2)}) collective-permute-start(s16[528,256]{1,0:T(8,128)(2,1)} %get-tuple-element.43), channel_id=1, source_target_pairs={{0,6},{2,4},{4,2},{6,0},{8,14},{10,12},{12,10},{14,8},{16,22},{18,... | collective-permute-start | bytes 811016 | tf_op jit(solution)/shard_map/ppermute | solution.py:526
  51.7 11.3 %copy-start.10 = (f32[512,256]{1,0:T(8,128)S(1)}, f32[512,256]{1,0:T(8,128)}, u32[]{:S(2)}) copy-start(f32[512,256]{1,0:T(8,128)} %get-tuple-element.40.own_ref) | copy-start | bytes 1572868
  58.4 5.3 %copy-start.1 = (s16[1280,256]{1,0:T(8,128)(2,1)}, s16[1280,256]{1,0:T(8,128)(2,1)S(1)}, u32[]{:S(2)}) copy-start(s16[1280,256]{1,0:T(8,128)(2,1)S(1)} %block_slots.1) | copy-start | bytes 1966084
  63.7 4.6 %collective-permute-start.4 = (s16[144,256]{1,0:T(8,128)(2,1)S(1)}, s16[144,256]{1,0:T(8,128)(2,1)S(1)}, u32[]{:S(2)}, u32[]{:S(2)}) collective-permute-start(s16[144,256]{1,0:T(8,128)(2,1)S(1)} %get-tuple-element.45), channel_id=1, source_target_pairs={{0,8},{2,10},{4,12},{6,14},{8,0},{10,2},{12,4},{14,6},{16,24},{18,... | collective-permute-start | bytes 221192 | tf_op jit(solution)/shard_map/ppermute | solution.py:526
  65.2 6.3 %collective-permute-start.5 = (s16[144,256]{1,0:T(8,128)(2,1)S(1)}, s16[144,256]{1,0:T(8,128)(2,1)S(1)}, u32[]{:S(2)}, u32[]{:S(2)}) collective-permute-start(s16[144,256]{1,0:T(8,128)(2,1)S(1)} %get-tuple-element.46), channel_id=1, source_target_pairs={{0,16},{2,18},{4,20},{6,22},{8,24},{10,26},{12,28},{14,30},{16,0},... | collective-permute-start | bytes 221192 | tf_op jit(solution)/shard_map/ppermute | solution.py:526
  67.6 6.7 %collective-permute-start.6 = (s16[144,256]{1,0:T(8,128)(2,1)S(1)}, s16[144,256]{1,0:T(8,128)(2,1)S(1)}, u32[]{:S(2)}, u32[]{:S(2)}) collective-permute-start(s16[144,256]{1,0:T(8,128)(2,1)S(1)} %get-tuple-element.47), channel_id=1, source_target_pairs={{0,24},{2,26},{4,28},{6,30},{8,16},{10,18},{12,20},{14,22},{16,8},... | collective-permute-start | bytes 221192 | tf_op jit(solution)/shard_map/ppermute | solution.py:526
  68.1 34.0 %collective-permute-start.13 = (f32[2048,256]{1,0:T(8,128)}, f32[2048,256]{1,0:T(8,128)}, u32[]{:S(2)}, u32[]{:S(2)}) collective-permute-start(f32[2048,256]{1,0:T(8,128)} %get-tuple-element.52), channel_id=1, source_target_pairs={{0,1},{1,0},{2,3},{3,2},{4,5},{5,4},{6,7},{7,6},{8,9},{9,8},{10,11... | collective-permute-start | bytes 6291464 | tf_op jit(solution)/shard_map/ppermute | solution.py:532
  74.3 26.6 %copy-start.5 = (s32[16,1,128]{2,1,0:T(1,128)S(1)}, s32[16,1,128]{2,1,0:T(1,128)}, u32[]{:S(2)}) copy-start(s32[16,1,128]{2,1,0:T(1,128)} %copy-done.4) | copy-start | bytes 24580
  74.3 27.8 %copy-start = (f32[2048,256]{1,0:T(8,128)S(1)}, f32[2048,256]{1,0:T(8,128)}, u32[]{:S(2)}) copy-start(f32[2048,256]{1,0:T(8,128)} %get-tuple-element.51.refs_4_) | copy-start | bytes 6291460
  74.6 4.5 %collective-permute-start.7 = (s16[144,256]{1,0:T(8,128)(2,1)S(1)}, s16[144,256]{1,0:T(8,128)(2,1)S(1)}, u32[]{:S(2)}, u32[]{:S(2)}) collective-permute-start(s16[144,256]{1,0:T(8,128)(2,1)S(1)} %sum_line.1), channel_id=1, source_target_pairs={{0,8},{2,10},{4,12},{6,14},{8,0},{10,2},{12,4},{14,6},{16,24},{18,... | collective-permute-start | bytes 221192 | tf_op jit(solution)/shard_map/ppermute | solution.py:526
  74.7 5.3 %collective-permute-start.8 = (s16[144,256]{1,0:T(8,128)(2,1)S(1)}, s16[144,256]{1,0:T(8,128)(2,1)S(1)}, u32[]{:S(2)}, u32[]{:S(2)}) collective-permute-start(s16[144,256]{1,0:T(8,128)(2,1)S(1)} %sum_line.1), channel_id=1, source_target_pairs={{0,16},{2,18},{4,20},{6,22},{8,24},{10,26},{12,28},{14,30},{16,0},... | collective-permute-start | bytes 221192 | tf_op jit(solution)/shard_map/ppermute | solution.py:526
  75.6 6.7 %collective-permute-start.9 = (s16[144,256]{1,0:T(8,128)(2,1)S(1)}, s16[144,256]{1,0:T(8,128)(2,1)S(1)}, u32[]{:S(2)}, u32[]{:S(2)}) collective-permute-start(s16[144,256]{1,0:T(8,128)(2,1)S(1)} %sum_line.1), channel_id=1, source_target_pairs={{0,24},{2,26},{4,28},{6,30},{8,16},{10,18},{12,20},{14,22},{16,8},... | collective-permute-start | bytes 221192 | tf_op jit(solution)/shard_map/ppermute | solution.py:526
  82.3 17.4 %all-to-all-start.2 = ((s16[16,80,256]{2,1,0:T(8,128)(2,1)}), s16[16,80,256]{2,1,0:T(8,128)(2,1)S(1)}, u32[]{:S(2)}, u32[]{:S(2)}) async-start(s16[16,80,256]{2,1,0:T(8,128)(2,1)} %bitcast.18), calls=%async_computation.2 | async-start | bytes 1310720 | tf_op jit(solution)/shard_map/all_to_all | solution.py:529
  87.5 10.2 %collective-permute-start.10 = (s16[576,256]{1,0:T(8,128)(2,1)S(1)}, s16[576,256]{1,0:T(8,128)(2,1)S(1)}, u32[]{:S(2)}, u32[]{:S(2)}) collective-permute-start(s16[576,256]{1,0:T(8,128)(2,1)S(1)} %pad_add_fusion.refs_0_), channel_id=1, source_target_pairs={{0,2},{2,0},{4,6},{6,4},{8,10},{10,8},{12,14},{14,12},{16,18},{18,... | collective-permute-start | bytes 884744 | tf_op jit(solution)/shard_map/ppermute | solution.py:526
  89.5 8.6 %collective-permute-start.11 = (s16[576,256]{1,0:T(8,128)(2,1)S(1)}, s16[576,256]{1,0:T(8,128)(2,1)S(1)}, u32[]{:S(2)}, u32[]{:S(2)}) collective-permute-start(s16[576,256]{1,0:T(8,128)(2,1)S(1)} %pad_add_fusion.refs_0_), channel_id=1, source_target_pairs={{0,4},{2,6},{4,0},{6,2},{8,12},{10,14},{12,8},{14,10},{16,20},{18,... | collective-permute-start | bytes 884744 | tf_op jit(solution)/shard_map/ppermute | solution.py:526
  98.1 0.7 copy-start.2
  99.8 2.4 %collective-permute-start.12 = (s16[1280,256]{1,0:T(8,128)(2,1)S(1)}, s16[1280,256]{1,0:T(8,128)(2,1)S(1)}, u32[]{:S(2)}, u32[]{:S(2)}) collective-permute-start(s16[1280,256]{1,0:T(8,128)(2,1)S(1)} %bitcast.16), channel_id=1, source_target_pairs={{0,1},{1,0},{2,3},{3,2},{4,5},{5,4},{6,7},{7,6},{8,9},{9,8},{10,11... | collective-permute-start | bytes 1966088 | tf_op jit(solution)/shard_map/ppermute | solution.py:532
  99.8 10.3 %collective-permute-start.14 = (s16[576,256]{1,0:T(8,128)(2,1)S(1)}, s16[576,256]{1,0:T(8,128)(2,1)S(1)}, u32[]{:S(2)}, u32[]{:S(2)}) collective-permute-start(s16[576,256]{1,0:T(8,128)(2,1)S(1)} %pad_add_fusion.refs_0_), channel_id=1, source_target_pairs={{0,6},{2,4},{4,2},{6,0},{8,14},{10,12},{12,10},{14,8},{16,22},{18,... | collective-permute-start | bytes 884744 | tf_op jit(solution)/shard_map/ppermute | solution.py:526
  100.9 1.2 %collective-permute-start = (s32[16,128]{1,0:T(8,128)S(1)}, s32[16,128]{1,0:T(8,128)S(1)}, u32[]{:S(2)}, u32[]{:S(2)}) collective-permute-start(s32[16,128]{1,0:T(8,128)S(1)} %bitcast.21), channel_id=1, source_target_pairs={{0,1},{1,0},{2,3},{3,2},{4,5},{5,4},{6,7},{7,6},{8,9},{9,8},{10,11... | collective-permute-start | bytes 24584 | tf_op jit(solution)/shard_map/ppermute | solution.py:532
  102.1 8.0 %copy-start.3 = (s16[576,256]{1,0:T(8,128)(2,1)S(1)}, s16[576,256]{1,0:T(8,128)(2,1)}, u32[]{:S(2)}) copy-start(s16[576,256]{1,0:T(8,128)(2,1)} %copy-done.2) | copy-start | bytes 884740
